TPU v7x, 32 devices: a whole 2x2x4 slice. The times are simulated.
32 devices in a mesh: param: 4 (over y, x), slab: 8 (over z, core).
Axes of the slice: x: 2, y: 2, z: 4, core: 2. Of those that a mesh axis runs over, the one named last changes fastest.
Arguments:
- init_state: float32 [4, 128, 128, 128], P('param', None, 'slab'), may hold values from -6 to 6
- coef: float32 [4, 128, 128], P('param', 'slab'), may hold values from 0.06 to 0.16
- source: float32 [128, 128], P('slab'), may hold values from -6 to 6
- amplitudes: float32 [64], replicated, may hold values from 0.5 to 2
- sample_idx: int32 [4, 128], P('param'), may hold values from 0 to 63
- step_counts: int32 [4], P('param'), may hold values from 1 to 8, as said below
- sketch_signs: int32 [3, 128, 64], replicated, may hold values from 0 to 1
Outputs:
- modes: float32 [64, 128, 128], P(None, 'slab', 'param')
Inputs may be any that keep to these rules, and one draw needn't show every extreme that they name: `step_counts`: one group takes all 8 steps and another exactly one.
All inputs are finite; a program needn't handle non-finite values.
Results may differ from a plain program's by a relative error of at most 0.0003.
Values sent between devices are 32-bit elements; how exact they have to be, the bound alone decides.
A program may use at most 64 MiB of HBM per device.

v0:
```python
import math

import jax
import jax.numpy as jnp
from jax import lax
from jax.sharding import PartitionSpec as P

STEPS = 8


def with_halo(value, sides, width):
    for axis, dim in sides:
        peers, length = (lax.axis_size(axis), value.shape[dim])
        up = [(i, (i + 1) % peers) for i in range(peers - 1)]
        down = [(j, i) for i, j in up]
        last = lax.slice_in_dim(value, length - width, length, axis=dim)
        first = lax.slice_in_dim(value, 0, width, axis=dim)
        before = lax.ppermute(last, axis, up)
        after = lax.ppermute(first, axis, down)
        value = jnp.concatenate([before, value, after], axis=dim)
    return value


def omega_rows(sketch_signs, level):
    signs = sketch_signs[level].astype(jnp.float32)
    return (2.0 * signs - 1.0).T / math.sqrt(sketch_signs.shape[1])


def compress(stacked, gram, omega_t):
    highest = lax.Precision.HIGHEST
    modes_kept = omega_t.shape[0]
    ident = jnp.eye(modes_kept, dtype=jnp.float32)
    moment = jnp.dot(jnp.dot(omega_t, gram, precision=highest), omega_t.T, precision=highest)
    moment = moment + 0.0001 * jnp.trace(moment) / modes_kept * ident
    lower = jnp.linalg.cholesky(moment)
    left = jax.scipy.linalg.solve_triangular(lower, omega_t, lower=True)
    hmat = jnp.dot(left, gram, precision=highest)
    inner = jnp.dot(hmat, hmat.T, precision=highest)
    inner = inner + 0.0001 * jnp.trace(inner) / modes_kept * ident
    factor = jnp.linalg.cholesky(inner)
    mixing = jnp.dot(factor.T, left, precision=highest)
    return (jnp.dot(mixing, stacked, precision=highest), mixing)


def piece_gram(mixing, gram):
    highest = lax.Precision.HIGHEST
    return jnp.dot(jnp.dot(mixing, gram, precision=highest), mixing.T, precision=highest)


def per_device(init_state, coef, source, amplitudes, sample_idx, step_counts, sketch_signs):
    highest = lax.Precision.HIGHEST
    field = init_state[0]
    snaps, rows, cols = field.shape
    table = amplitudes.shape[0]
    picks = sample_idx[0][:, None] == jnp.arange(table, dtype=jnp.int32)[None, :]
    amp = jnp.sum(jnp.where(picks, amplitudes[None, :], 0.0), axis=1)
    forcing = 0.1 * amp[:, None, None] * source[None]
    rate_base = coef[0]
    count = step_counts[0]
    for step in range(STEPS):
        padded = with_halo(field, (("slab", 1),), 1)
        beside = jnp.pad(field, ((0, 0), (0, 0), (1, 1)))
        lap = padded[:, 2:] + padded[:, :-2] + beside[:, :, 2:] + beside[:, :, :-2] - 4.0 * field
        new = field + rate_base * (1.0 + 0.5 * jnp.tanh(field) ** 2) * lap + forcing
        field = jnp.where(step < count, new, field)
    stacked = field.reshape(snaps, rows * cols)
    gram = lax.psum(jnp.dot(stacked, stacked.T, precision=highest), "slab")
    piece, mixing = compress(stacked, gram, omega_rows(sketch_signs, 0))
    own_gram = piece_gram(mixing, gram)
    levels = lax.axis_size("param").bit_length() - 1
    place = lax.axis_index("param")
    scale_half = 0.5**0.5
    pieces, grams = (
        lax.all_gather(piece[None], "param", axis=0, tiled=True),
        lax.all_gather(own_gram[None], "param", axis=0, tiled=True),
    )
    for level in range(levels):
        firsts = pieces[0::2]
        seconds = pieces[1::2]
        stacked = jnp.concatenate([firsts, seconds], axis=1) * scale_half
        cross = lax.psum(jnp.einsum("pac,pbc->pab", firsts, seconds, precision=highest), "slab")
        top = jnp.concatenate([grams[0::2], cross], axis=2)
        bottom = jnp.concatenate([jnp.swapaxes(cross, 1, 2), grams[1::2]], axis=2)
        gram = 0.5 * jnp.concatenate([top, bottom], axis=1)
        omega_t = omega_rows(sketch_signs, level + 1)
        pieces, mixings = jax.vmap(compress, in_axes=(0, 0, None))(stacked, gram, omega_t)
        grams = jax.vmap(piece_gram)(mixings, gram)
    piece = pieces[0]
    whole = piece.reshape(piece.shape[0], rows, cols)
    width = cols // lax.axis_size("param")
    return lax.dynamic_slice_in_dim(whole, place * width, width, 2)


def solution(mesh):
    return jax.shard_map(
        per_device,
        mesh=mesh,
        in_specs=(
            P("param", None, "slab", None),
            P("param", "slab", None),
            P("slab", None),
            P(),
            P("param", None),
            P("param"),
            P(),
        ),
        out_specs=P(None, "slab", "param"),
        check_vma=False,
    )
```

profile of v0, /device:TPU:0, one launch (start us, length us, event | category | flops | bytes accessed | tf_op | source)
XLA Modules:
  0.0 330.4 jit_solution(15775988643753042228)
XLA Ops:
  9.2 3.0 collective-permute-start.1
  13.6 3.8 %fusion.8 = f32[128,16,128]{2,1,0:T(8,128)S(1)} fusion(f32[128,16,128]{2,1,0:T(8,128)} %bitcast.153, f32[128,1,128]{2,1,0:T(1,128)S(1)} %collective-permute-done.1, f32[128,1,128]{2,1,0:T(1,128)S(1)} %collective-permute-done, f32[16,128]{1,0:T(8,128)} %param.12, f32[128]{0:T(128)S(1)} %broadcast_multiply_fusion.2, f32[16,128]{1,0:T(8,128)} %bitcast.154, ...), kind=kLoop, calls=%fused_computation.37 | loop fusion | flops 4194304 | bytes 2245121 | tf_op jit(solution)/shard_map/jit(_where)/select_n | solution.py:65
  18.9 5.2 %collective-permute-start.3 = (f32[128,1,128]{2,1,0:T(1,128)S(1)}, f32[128,1,128]{2,1,0:T(1,128)S(1)}, u32[]{:S(2)}, u32[]{:S(2)}) collective-permute-start(f32[128,1,128]{2,1,0:T(1,128)S(1)} %get-tuple-element.25), channel_id=1, source_target_pairs={{0,1},{1,2},{2,3},{3,4},{4,5},{5,6},{6,7},{8,9},{9,10},{10,11},{11... | collective-permute-start | bytes 196616 | tf_op jit(solution)/shard_map/ppermute | solution.py:18
  27.4 5.2 %collective-permute-start.5 = (f32[128,1,128]{2,1,0:T(1,128)S(1)}, f32[128,1,128]{2,1,0:T(1,128)S(1)}, u32[]{:S(2)}, u32[]{:S(2)}) collective-permute-start(f32[128,1,128]{2,1,0:T(1,128)S(1)} %get-tuple-element.23), channel_id=1, source_target_pairs={{0,1},{1,2},{2,3},{3,4},{4,5},{5,6},{6,7},{8,9},{9,10},{10,11},{11... | collective-permute-start | bytes 196616 | tf_op jit(solution)/shard_map/ppermute | solution.py:18
  36.0 5.3 %collective-permute-start.7 = (f32[128,1,128]{2,1,0:T(1,128)S(1)}, f32[128,1,128]{2,1,0:T(1,128)S(1)}, u32[]{:S(2)}, u32[]{:S(2)}) collective-permute-start(f32[128,1,128]{2,1,0:T(1,128)S(1)} %get-tuple-element.21), channel_id=1, source_target_pairs={{0,1},{1,2},{2,3},{3,4},{4,5},{5,6},{6,7},{8,9},{9,10},{10,11},{11... | collective-permute-start | bytes 196616 | tf_op jit(solution)/shard_map/ppermute | solution.py:18
  44.7 5.3 %collective-permute-start.9 = (f32[128,1,128]{2,1,0:T(1,128)S(1)}, f32[128,1,128]{2,1,0:T(1,128)S(1)}, u32[]{:S(2)}, u32[]{:S(2)}) collective-permute-start(f32[128,1,128]{2,1,0:T(1,128)S(1)} %get-tuple-element.19), channel_id=1, source_target_pairs={{0,1},{1,2},{2,3},{3,4},{4,5},{5,6},{6,7},{8,9},{9,10},{10,11},{11... | collective-permute-start | bytes 196616 | tf_op jit(solution)/shard_map/ppermute | solution.py:18
  53.4 5.3 %collective-permute-start.11 = (f32[128,1,128]{2,1,0:T(1,128)S(1)}, f32[128,1,128]{2,1,0:T(1,128)S(1)}, u32[]{:S(2)}, u32[]{:S(2)}) collective-permute-start(f32[128,1,128]{2,1,0:T(1,128)S(1)} %get-tuple-element.17), channel_id=1, source_target_pairs={{0,1},{1,2},{2,3},{3,4},{4,5},{5,6},{6,7},{8,9},{9,10},{10,11},{11... | collective-permute-start | bytes 196616 | tf_op jit(solution)/shard_map/ppermute | solution.py:18
  62.1 5.3 %collective-permute-start.13 = (f32[128,1,128]{2,1,0:T(1,128)S(1)}, f32[128,1,128]{2,1,0:T(1,128)S(1)}, u32[]{:S(2)}, u32[]{:S(2)}) collective-permute-start(f32[128,1,128]{2,1,0:T(1,128)S(1)} %get-tuple-element.15), channel_id=1, source_target_pairs={{0,1},{1,2},{2,3},{3,4},{4,5},{5,6},{6,7},{8,9},{9,10},{10,11},{11... | collective-permute-start | bytes 196616 | tf_op jit(solution)/shard_map/ppermute | solution.py:18
  70.8 5.5 %collective-permute-start.15 = (f32[128,1,128]{2,1,0:T(1,128)S(1)}, f32[128,1,128]{2,1,0:T(1,128)S(1)}, u32[]{:S(2)}, u32[]{:S(2)}) collective-permute-start(f32[128,1,128]{2,1,0:T(1,128)S(1)} %get-tuple-element.13), channel_id=1, source_target_pairs={{0,1},{1,2},{2,3},{3,4},{4,5},{5,6},{6,7},{8,9},{9,10},{10,11},{11... | collective-permute-start | bytes 196616 | tf_op jit(solution)/shard_map/ppermute | solution.py:18
  78.1 2.1 convolution_bitcast_fusion.1
  80.3 58.4 %all-reduce.10.cloned.1.call-done = f32[128,128]{1,0:T(8,128)} async-done(((f32[128,128]{1,0:T(8,128)}), f32[128,128]{1,0:T(8,128)}) %all-reduce.10.cloned.1.call-update) | async-done | bytes 65552 | tf_op jit(solution)/shard_map/psum | solution.py:67
  141.4 5.8 %cholesky.127 = f32[64,64]{1,0:T(8,128)S(1)} custom-call(f32[64,64]{1,0:T(8,128)S(1)} %fusion.85), custom_call_target="Cholesky" | custom-call | tf_op jit(solution)/shard_map/jit(cholesky)/cholesky | solution.py:35
  148.8 4.9 %custom-call.20 = f32[1,64,64]{1,2,0:T(8,128)S(1)} custom-call(f32[1,64,64]{2,1,0:T(8,128)S(1)} %copy.47), custom_call_target="InvertDiagBlocksLowerTriangular" | custom-call | tf_op jit(solution)/shard_map/jit(_solve_triangular)/triangular_solve | solution.py:36
  156.6 5.8 %cholesky.138 = f32[64,64]{1,0:T(8,128)S(1)} custom-call(f32[64,64]{1,0:T(8,128)S(1)} %fusion.82), custom_call_target="Cholesky" | custom-call | tf_op jit(solution)/shard_map/jit(cholesky)/cholesky | solution.py:40
  166.3 8.4 %all-gather = f32[256,64]{1,0:T(8,128)S(1)} all-gather(f32[64,64]{1,0:T(8,128)S(1)} %fusion.218), channel_id=2, replica_groups=mesh['param'=4,'slab'=8] {'param'}, dimensions={0}, use_global_device_ids=true | all-gather | bytes 81920 | tf_op jit(solution)/shard_map/all_gather | solution.py:75
  174.9 25.4 %all-gather.4.cloned.1.call-done = f32[256,2048]{1,0:T(8,128)} async-done(((f32[64,2048]{1,0:T(8,128)}), f32[256,2048]{1,0:T(8,128)}) %all-gather.4.cloned.1.call-update) | async-done | bytes 2097168 | tf_op jit(solution)/shard_map/all_gather | solution.py:74
  203.6 29.0 %psum.22 = f32[2,64,64]{2,1,0:T(8,128)S(1)} all-reduce(f32[2,64,64]{2,1,0:T(8,128)S(1)} %fusion.200), channel_id=1, replica_groups=mesh['param'=4,'slab'=8] {'slab'}, use_global_device_ids=true, to_apply=%region_6.8 | all-reduce | flops 8192 | bytes 65536 | tf_op jit(solution)/shard_map/psum | solution.py:81
  233.7 11.7 %custom-call.25 = f32[2,64,64]{2,1,0:T(8,128)S(1)} custom-call(f32[2,64,64]{2,1,0:T(8,128)S(1)} %fusion.68), custom_call_target="Cholesky" | custom-call | tf_op jit(solution)/shard_map/vmap(jit(cholesky))/cholesky | solution.py:35
  245.9 9.8 %custom-call.21 = f32[2,1,64,64]{2,3,1,0:T(8,128)S(1)} custom-call(f32[2,1,64,64]{3,2,1,0:T(8,128)S(1)} %copy.58), custom_call_target="InvertDiagBlocksLowerTriangular" | custom-call | tf_op jit(solution)/shard_map/vmap(jit(_solve_triangular))/triangular_solve | solution.py:36
  257.1 11.7 %custom-call.26 = f32[2,64,64]{2,1,0:T(8,128)S(1)} custom-call(f32[2,64,64]{2,1,0:T(8,128)S(1)} %fusion.65), custom_call_target="Cholesky" | custom-call | tf_op jit(solution)/shard_map/vmap(jit(cholesky))/cholesky | solution.py:40
  272.5 25.9 %psum.23 = f32[1,64,64]{2,1,0:T(8,128)S(1)} all-reduce(f32[1,64,64]{2,1,0:T(8,128)S(1)} %convolution_bitcast_fusion.3), channel_id=1, replica_groups=mesh['param'=4,'slab'=8] {'slab'}, use_global_device_ids=true, to_apply=%region_11.14 | all-reduce | flops 4096 | bytes 32768 | tf_op jit(solution)/shard_map/psum | solution.py:81
  300.4 5.8 %custom-call.27 = f32[1,64,64]{2,1,0:T(8,128)S(1)} custom-call(f32[1,64,64]{2,1,0:T(8,128)S(1)} %fusion.78), custom_call_target="Cholesky" | custom-call | tf_op jit(solution)/shard_map/vmap(jit(cholesky))/cholesky | solution.py:35
  307.6 4.9 %custom-call.22 = f32[1,1,64,64]{2,3,1,0:T(8,128)S(1)} custom-call(f32[1,1,64,64]{3,2,1,0:T(8,128)S(1)} %fusion.76), custom_call_target="InvertDiagBlocksLowerTriangular" | custom-call | tf_op jit(solution)/shard_map/vmap(jit(_solve_triangular))/triangular_solve | solution.py:36
  314.5 5.8 %custom-call.28 = f32[1,64,64]{2,1,0:T(8,128)S(1)} custom-call(f32[1,64,64]{2,1,0:T(8,128)S(1)} %fusion.77), custom_call_target="Cholesky" | custom-call | tf_op jit(solution)/shard_map/vmap(jit(cholesky))/cholesky | solution.py:40
  (139 shorter events, 53.2 us)
Async XLA Ops:
  6.5 18.4 %copy-start.4 = (f32[1,16,128]{2,1,0:T(8,128)S(1)}, f32[1,16,128]{2,1,0:T(8,128)}, u32[]{:S(2)}) copy-start(f32[1,16,128]{2,1,0:T(8,128)} %param.11) | copy-start | bytes 24580
  6.5 18.4 %copy-start.3 = (f32[16,128]{1,0:T(8,128)S(1)}, f32[16,128]{1,0:T(8,128)}, u32[]{:S(2)}) copy-start(f32[16,128]{1,0:T(8,128)} %param.12) | copy-start | bytes 24580
  6.5 132.2 %all-reduce.10.cloned.1.call-start = ((), (), s32[]{:S(2)}) async-start(), calls=%async_computation | async-start | bytes 131072 | tf_op jit(solution)/shard_map/psum | solution.py:67
  7.9 5.8 %collective-permute-start = (f32[128,1,128]{2,1,0:T(1,128)S(1)}, f32[128,1,128]{2,1,0:T(1,128)S(1)}, u32[]{:S(2)}, u32[]{:S(2)}) collective-permute-start(f32[128,1,128]{2,1,0:T(1,128)S(1)} %get-tuple-element.26), channel_id=1, source_target_pairs={{1,0},{2,1},{3,2},{4,3},{5,4},{6,5},{7,6},{9,8},{10,9},{11,10},{12... | collective-permute-start | bytes 196616 | tf_op jit(solution)/shard_map/ppermute | solution.py:19
  9.2 4.5 %collective-permute-start.1 = (f32[128,1,128]{2,1,0:T(1,128)S(1)}, f32[128,1,128]{2,1,0:T(1,128)S(1)}, u32[]{:S(2)}, u32[]{:S(2)}) collective-permute-start(f32[128,1,128]{2,1,0:T(1,128)S(1)} %get-tuple-element.27), channel_id=1, source_target_pairs={{0,1},{1,2},{2,3},{3,4},{4,5},{5,6},{6,7},{8,9},{9,10},{10,11},{11... | collective-permute-start | bytes 196616 | tf_op jit(solution)/shard_map/ppermute | solution.py:18
  17.6 6.5 %collective-permute-start.2 = (f32[128,1,128]{2,1,0:T(1,128)S(1)}, f32[128,1,128]{2,1,0:T(1,128)S(1)}, u32[]{:S(2)}, u32[]{:S(2)}) collective-permute-start(f32[128,1,128]{2,1,0:T(1,128)S(1)} %get-tuple-element.24), channel_id=1, source_target_pairs={{1,0},{2,1},{3,2},{4,3},{5,4},{6,5},{7,6},{9,8},{10,9},{11,10},{12... | collective-permute-start | bytes 196616 | tf_op jit(solution)/shard_map/ppermute | solution.py:19
  18.9 6.1 %collective-permute-start.3 = (f32[128,1,128]{2,1,0:T(1,128)S(1)}, f32[128,1,128]{2,1,0:T(1,128)S(1)}, u32[]{:S(2)}, u32[]{:S(2)}) collective-permute-start(f32[128,1,128]{2,1,0:T(1,128)S(1)} %get-tuple-element.25), channel_id=1, source_target_pairs={{0,1},{1,2},{2,3},{3,4},{4,5},{5,6},{6,7},{8,9},{9,10},{10,11},{11... | collective-permute-start | bytes 196616 | tf_op jit(solution)/shard_map/ppermute | solution.py:18
  26.1 6.5 %collective-permute-start.4 = (f32[128,1,128]{2,1,0:T(1,128)S(1)}, f32[128,1,128]{2,1,0:T(1,128)S(1)}, u32[]{:S(2)}, u32[]{:S(2)}) collective-permute-start(f32[128,1,128]{2,1,0:T(1,128)S(1)} %get-tuple-element.22), channel_id=1, source_target_pairs={{1,0},{2,1},{3,2},{4,3},{5,4},{6,5},{7,6},{9,8},{10,9},{11,10},{12... | collective-permute-start | bytes 196616 | tf_op jit(solution)/shard_map/ppermute | solution.py:19
  27.4 6.1 %collective-permute-start.5 = (f32[128,1,128]{2,1,0:T(1,128)S(1)}, f32[128,1,128]{2,1,0:T(1,128)S(1)}, u32[]{:S(2)}, u32[]{:S(2)}) collective-permute-start(f32[128,1,128]{2,1,0:T(1,128)S(1)} %get-tuple-element.23), channel_id=1, source_target_pairs={{0,1},{1,2},{2,3},{3,4},{4,5},{5,6},{6,7},{8,9},{9,10},{10,11},{11... | collective-permute-start | bytes 196616 | tf_op jit(solution)/shard_map/ppermute | solution.py:18
  34.7 6.6 %collective-permute-start.6 = (f32[128,1,128]{2,1,0:T(1,128)S(1)}, f32[128,1,128]{2,1,0:T(1,128)S(1)}, u32[]{:S(2)}, u32[]{:S(2)}) collective-permute-start(f32[128,1,128]{2,1,0:T(1,128)S(1)} %get-tuple-element.20), channel_id=1, source_target_pairs={{1,0},{2,1},{3,2},{4,3},{5,4},{6,5},{7,6},{9,8},{10,9},{11,10},{12... | collective-permute-start | bytes 196616 | tf_op jit(solution)/shard_map/ppermute | solution.py:19
  36.0 6.2 %collective-permute-start.7 = (f32[128,1,128]{2,1,0:T(1,128)S(1)}, f32[128,1,128]{2,1,0:T(1,128)S(1)}, u32[]{:S(2)}, u32[]{:S(2)}) collective-permute-start(f32[128,1,128]{2,1,0:T(1,128)S(1)} %get-tuple-element.21), channel_id=1, source_target_pairs={{0,1},{1,2},{2,3},{3,4},{4,5},{5,6},{6,7},{8,9},{9,10},{10,11},{11... | collective-permute-start | bytes 196616 | tf_op jit(solution)/shard_map/ppermute | solution.py:18
  43.4 6.6 %collective-permute-start.8 = (f32[128,1,128]{2,1,0:T(1,128)S(1)}, f32[128,1,128]{2,1,0:T(1,128)S(1)}, u32[]{:S(2)}, u32[]{:S(2)}) collective-permute-start(f32[128,1,128]{2,1,0:T(1,128)S(1)} %get-tuple-element.18), channel_id=1, source_target_pairs={{1,0},{2,1},{3,2},{4,3},{5,4},{6,5},{7,6},{9,8},{10,9},{11,10},{12... | collective-permute-start | bytes 196616 | tf_op jit(solution)/shard_map/ppermute | solution.py:19
  44.7 6.2 %collective-permute-start.9 = (f32[128,1,128]{2,1,0:T(1,128)S(1)}, f32[128,1,128]{2,1,0:T(1,128)S(1)}, u32[]{:S(2)}, u32[]{:S(2)}) collective-permute-start(f32[128,1,128]{2,1,0:T(1,128)S(1)} %get-tuple-element.19), channel_id=1, source_target_pairs={{0,1},{1,2},{2,3},{3,4},{4,5},{5,6},{6,7},{8,9},{9,10},{10,11},{11... | collective-permute-start | bytes 196616 | tf_op jit(solution)/shard_map/ppermute | solution.py:18
  52.1 6.6 %collective-permute-start.10 = (f32[128,1,128]{2,1,0:T(1,128)S(1)}, f32[128,1,128]{2,1,0:T(1,128)S(1)}, u32[]{:S(2)}, u32[]{:S(2)}) collective-permute-start(f32[128,1,128]{2,1,0:T(1,128)S(1)} %get-tuple-element.16), channel_id=1, source_target_pairs={{1,0},{2,1},{3,2},{4,3},{5,4},{6,5},{7,6},{9,8},{10,9},{11,10},{12... | collective-permute-start | bytes 196616 | tf_op jit(solution)/shard_map/ppermute | solution.py:19
  53.4 6.2 %collective-permute-start.11 = (f32[128,1,128]{2,1,0:T(1,128)S(1)}, f32[128,1,128]{2,1,0:T(1,128)S(1)}, u32[]{:S(2)}, u32[]{:S(2)}) collective-permute-start(f32[128,1,128]{2,1,0:T(1,128)S(1)} %get-tuple-element.17), channel_id=1, source_target_pairs={{0,1},{1,2},{2,3},{3,4},{4,5},{5,6},{6,7},{8,9},{9,10},{10,11},{11... | collective-permute-start | bytes 196616 | tf_op jit(solution)/shard_map/ppermute | solution.py:18
  60.8 6.6 %collective-permute-start.12 = (f32[128,1,128]{2,1,0:T(1,128)S(1)}, f32[128,1,128]{2,1,0:T(1,128)S(1)}, u32[]{:S(2)}, u32[]{:S(2)}) collective-permute-start(f32[128,1,128]{2,1,0:T(1,128)S(1)} %get-tuple-element.14), channel_id=1, source_target_pairs={{1,0},{2,1},{3,2},{4,3},{5,4},{6,5},{7,6},{9,8},{10,9},{11,10},{12... | collective-permute-start | bytes 196616 | tf_op jit(solution)/shard_map/ppermute | solution.py:19
  62.1 6.2 %collective-permute-start.13 = (f32[128,1,128]{2,1,0:T(1,128)S(1)}, f32[128,1,128]{2,1,0:T(1,128)S(1)}, u32[]{:S(2)}, u32[]{:S(2)}) collective-permute-start(f32[128,1,128]{2,1,0:T(1,128)S(1)} %get-tuple-element.15), channel_id=1, source_target_pairs={{0,1},{1,2},{2,3},{3,4},{4,5},{5,6},{6,7},{8,9},{9,10},{10,11},{11... | collective-permute-start | bytes 196616 | tf_op jit(solution)/shard_map/ppermute | solution.py:18
  69.4 69.4 %copy-start.1 = (s32[3,128,64]{1,2,0:T(8,128)S(1)}, s32[3,128,64]{1,2,0:T(8,128)}, u32[]{:S(2)}) copy-start(s32[3,128,64]{1,2,0:T(8,128)} %param.16) | copy-start | bytes 294916
  69.5 6.8 %collective-permute-start.14 = (f32[128,1,128]{2,1,0:T(1,128)S(1)}, f32[128,1,128]{2,1,0:T(1,128)S(1)}, u32[]{:S(2)}, u32[]{:S(2)}) collective-permute-start(f32[128,1,128]{2,1,0:T(1,128)S(1)} %get-tuple-element.12), channel_id=1, source_target_pairs={{1,0},{2,1},{3,2},{4,3},{5,4},{6,5},{7,6},{9,8},{10,9},{11,10},{12... | collective-permute-start | bytes 196616 | tf_op jit(solution)/shard_map/ppermute | solution.py:19
  70.8 6.2 %collective-permute-start.15 = (f32[128,1,128]{2,1,0:T(1,128)S(1)}, f32[128,1,128]{2,1,0:T(1,128)S(1)}, u32[]{:S(2)}, u32[]{:S(2)}) collective-permute-start(f32[128,1,128]{2,1,0:T(1,128)S(1)} %get-tuple-element.13), channel_id=1, source_target_pairs={{0,1},{1,2},{2,3},{3,4},{4,5},{5,6},{6,7},{8,9},{9,10},{10,11},{11... | collective-permute-start | bytes 196616 | tf_op jit(solution)/shard_map/ppermute | solution.py:18
  80.3 120.0 %all-gather.4.cloned.1.call-start = ((), (), s32[]{:S(2)}) async-start(), calls=%async_computation.1 | async-start | bytes 2621440 | tf_op jit(solution)/shard_map/all_gather | solution.py:74
  138.7 27.2 %copy-start.2 = (f32[128,128]{1,0:T(8,128)S(1)}, f32[128,128]{1,0:T(8,128)}, u32[]{:S(2)}) copy-start(f32[128,128]{1,0:T(8,128)} %all-reduce.10.cloned.1.call-done) | copy-start | bytes 196612
  200.3 2.2 copy-start
Sparse Core Ops, SparseCore 0:
  80.4 58.3 all-reduce.9
  165.9 34.3 all-gather.3
where the time goes:
time: 331 us; the launch traced here: 330 us
  waiting for transfers between devices  89.7 us (27%)
  other arithmetic  83.8 us (25%)
  blocking collectives  63.3 us (19%)
  starting transfers between devices  50.6 us (15%)
  matrix products  19 us (6%)
  between operations  17.5 us (5%)
  local copies, waits for them, and re-layouts  6.44 us (2%)
    psum x1, waiting for transfers between devices, per_device(): gram = lax.psum(jnp.dot(stacked, stacked.T, precision=highest), 'slab')  58.4 us
    psum x2, blocking collectives, per_device(): lax.psum(jnp.einsum('pac,pbc->pab', firsts, seconds, precision=highest),...  54.9 us
    ppermute x8, starting transfers between devices, with_halo(): before = lax.ppermute(last, axis, up)  40.2 us
    all_gather x1, waiting for transfers between devices, per_device(): lax.all_gather(piece[None], 'param', axis=0, tiled=True)  25.4 us
    another operation x10, other arithmetic, compress(): lower = jnp.linalg.cholesky(moment)  25.1 us
    another operation x10, other arithmetic, compress(): factor = jnp.linalg.cholesky(inner)  24.9 us
    another operation x7, other arithmetic, compress(): left = jax.scipy.linalg.solve_triangular(lower, omega_t, lower=True)  21 us
    select_n x8, other arithmetic, per_device(): field = jnp.where(step < count, new, field)  11.3 us
  transfers between devices with their start and end apart: 18, of which 9 were waited for; matrix products, arithmetic and copies ran while one was open for 0% of the time, Pallas kernels for 0%

commit v1 on v0

v1 whole, which is shorter than its diff:
```python
import functools
import math

import jax
import jax.numpy as jnp
from jax import lax
from jax.experimental import pallas as pl
from jax.experimental.pallas import tpu as pltpu
from jax.sharding import PartitionSpec as P

STEPS = 8
MESH = pl.DeviceIdType.MESH
HIGHEST = lax.Precision.HIGHEST
VMEM_LIMIT = 48 * 1024 * 1024
VMEM = pl.BlockSpec(memory_space=pltpu.VMEM)
SMEM = pl.BlockSpec(memory_space=pltpu.SMEM)


def dot(a, b):
    return lax.dot_general(a, b, (((1,), (0,)), ((), ())), precision=HIGHEST, preferred_element_type=jnp.float32)


def dot_t(a, b):
    return lax.dot_general(a, b, (((1,), (1,)), ((), ())), precision=HIGHEST, preferred_element_type=jnp.float32)


def flow_kernel(slabs, x_ref, coef_ref, source_ref, table_ref, idx_ref, count_ref, field_ref, gram_ref,
                buf, halo, amp_ref, part, pieces, total, halo_send, halo_recv, rs_send, rs_recv, ag_send, ag_recv):
    rows, cols = coef_ref.shape
    snaps = gram_ref.shape[0]
    share = snaps // slabs
    me = lax.axis_index("slab")
    place = lax.axis_index("param")
    peers = [lax.rem(me + k, slabs) for k in range(1, slabs)]

    barrier = pltpu.get_barrier_semaphore()
    for peer in peers:
        pl.semaphore_signal(barrier, inc=1, device_id=(place, peer), device_id_type=MESH)

    for r in range(rows):
        buf[0, r] = x_ref[pl.ds(r, snaps, stride=rows), :]

    table = jnp.broadcast_to(table_ref[...], (8, table_ref.shape[1]))
    entry = lax.broadcasted_iota(jnp.int32, (table_ref.shape[1], snaps), 0)
    picks = jnp.where(entry == idx_ref[...], 1.0, 0.0)
    amp_row = 0.1 * dot(table, picks)[0:1]
    amp_ref[...] = jnp.transpose(jnp.broadcast_to(amp_row, (cols, snaps)))

    @pl.when(me == 0)
    def _():
        for step in range(STEPS):
            halo[step, 0] = jnp.zeros((snaps, cols), jnp.float32)

    @pl.when(me == slabs - 1)
    def _():
        for step in range(STEPS):
            halo[step, 1] = jnp.zeros((snaps, cols), jnp.float32)

    pl.semaphore_wait(barrier, slabs - 1)

    def down(step):
        return pltpu.make_async_remote_copy(
            src_ref=buf.at[step % 2, rows - 1], dst_ref=halo.at[step, 0],
            send_sem=halo_send.at[step, 0], recv_sem=halo_recv.at[step, 0],
            device_id=(place, lax.rem(me + 1, slabs)), device_id_type=MESH)

    def up(step):
        return pltpu.make_async_remote_copy(
            src_ref=buf.at[step % 2, 0], dst_ref=halo.at[step, 1],
            send_sem=halo_send.at[step, 1], recv_sem=halo_recv.at[step, 1],
            device_id=(place, lax.rem(me + slabs - 1, slabs)), device_id_type=MESH)

    def send(step):
        @pl.when(me < slabs - 1)
        def _():
            down(step).start()

        @pl.when(me > 0)
        def _():
            up(step).start()

    count = count_ref[0]
    chunk = 32
    lane = lax.broadcasted_iota(jnp.int32, (chunk, cols), 1)
    first, last = lane == 0, lane == cols - 1

    def update(step, r, above, below):
        now, later = step % 2, (step + 1) % 2
        active = jnp.where(step < count, 1.0, 0.0)
        rate = coef_ref[pl.ds(r, 1), :] * active
        force = source_ref[pl.ds(r, 1), :] * active
        for c in range(0, snaps, chunk):
            part_rows = pl.ds(c, chunk)
            f = buf[now, r, part_rows]
            left = jnp.where(first, 0.0, pltpu.roll(f, 1, 1))
            right = jnp.where(last, 0.0, pltpu.roll(f, cols - 1, 1))
            lap = below(part_rows) + above(part_rows) + right + left - 4.0 * f
            th = jnp.tanh(f)
            new = f + rate * (1.0 + 0.5 * (th * th)) * lap + amp_ref[part_rows] * force
            buf[later, r, part_rows] = new

    send(0)
    for step in range(STEPS):
        now = step % 2

        def inner(r, carry):
            update(step, r, lambda s: buf[now, r - 1, s], lambda s: buf[now, r + 1, s])
            return carry

        lax.fori_loop(1, rows - 1, inner, 0)

        @pl.when(me > 0)
        def _():
            down(step).wait_recv()
            up(step).wait_send()

        @pl.when(me < slabs - 1)
        def _():
            up(step).wait_recv()
            down(step).wait_send()

        update(step, 0, lambda s: halo[step, 0, s], lambda s: buf[now, 1, s])
        update(step, rows - 1, lambda s: buf[now, rows - 2, s], lambda s: halo[step, 1, s])
        if step < STEPS - 1:
            send(step + 1)

    end = STEPS % 2

    def products(i, acc):
        pair = jnp.concatenate([buf[end, 2 * i], buf[end, 2 * i + 1]], axis=1)
        return acc + dot_t(pair, pair)

    part[...] = lax.fori_loop(0, rows // 2, products, jnp.zeros((snaps, snaps), jnp.float32))

    def scatter(k):
        peer = lax.rem(me + k, slabs)
        return pltpu.make_async_remote_copy(
            src_ref=part.at[pl.ds(peer * share, share)], dst_ref=pieces.at[k],
            send_sem=rs_send.at[k], recv_sem=rs_recv.at[k], device_id=(place, peer), device_id_type=MESH)

    def gather(k):
        peer = lax.rem(me + k, slabs)
        return pltpu.make_async_remote_copy(
            src_ref=total, dst_ref=gram_ref.at[pl.ds(me * share, share)],
            send_sem=ag_send.at[k], recv_sem=ag_recv.at[k], device_id=(place, peer), device_id_type=MESH)

    for k in range(1, slabs):
        scatter(k).start()
    for r in range(rows):
        field_ref[r] = buf[end, r]
    acc = part[pl.ds(pl.multiple_of(me * share, 8), share)]
    for k in range(1, slabs):
        scatter(k).wait_recv()
        acc = acc + pieces[k]
    total[...] = acc
    for k in range(1, slabs):
        gather(k).start()
    gram_ref[pl.ds(pl.multiple_of(me * share, 8), share)] = acc
    for k in range(1, slabs):
        scatter(k).wait_send()
    for k in range(1, slabs):
        gather(k).wait()


def flow(slabs, x, coef, source, table, idx, count):
    rows, cols = coef.shape
    snaps = x.shape[0] // rows
    f32 = jnp.float32
    return pl.pallas_call(
        functools.partial(flow_kernel, slabs),
        out_shape=(jax.ShapeDtypeStruct((rows, snaps, cols), f32), jax.ShapeDtypeStruct((snaps, snaps), f32)),
        in_specs=[VMEM, VMEM, VMEM, VMEM, VMEM, SMEM],
        out_specs=(VMEM, VMEM),
        scratch_shapes=[
            pltpu.VMEM((2, rows, snaps, cols), f32),
            pltpu.VMEM((STEPS, 2, snaps, cols), f32),
            pltpu.VMEM((snaps, cols), f32),
            pltpu.VMEM((snaps, snaps), f32),
            pltpu.VMEM((slabs, snaps // slabs, snaps), f32),
            pltpu.VMEM((snaps // slabs, snaps), f32),
            pltpu.SemaphoreType.DMA((STEPS, 2)),
            pltpu.SemaphoreType.DMA((STEPS, 2)),
            pltpu.SemaphoreType.DMA((slabs,)),
            pltpu.SemaphoreType.DMA((slabs,)),
            pltpu.SemaphoreType.DMA((slabs,)),
            pltpu.SemaphoreType.DMA((slabs,)),
        ],
        compiler_params=pltpu.CompilerParams(collective_id=0, has_side_effects=True, vmem_limit_bytes=VMEM_LIMIT),
    )(x, coef, source, table, idx, count)


def eliminate(problems, outs):
    size = problems[0][0].shape[0]
    blocks = size // 8
    wide = 128
    sub = lax.broadcasted_iota(jnp.int32, (8, wide), 0)
    lane = lax.broadcasted_iota(jnp.int32, (8, wide), 1)

    def split(value):
        return tuple(value[8 * b : 8 * b + 8] for b in range(blocks))

    def padded(m):
        return jnp.concatenate([m, jnp.zeros((size, wide - size), jnp.float32)], axis=1)

    start = tuple((split(padded(m)), split(r)) for m, r in problems)

    def body(t, carry):
        states = [[list(ms), list(rs)] for ms, rs in carry]
        for k in range(8):
            for ms, rs in states:
                inv = 1.0 / ms[0][k : k + 1, k : k + 1]
                row_m = ms[0][k : k + 1] * inv
                row_r = rs[0][k : k + 1] * inv
                cols = [jnp.broadcast_to(ms[b][:, k : k + 1], (8, wide)) for b in range(blocks)]
                cols[0] = jnp.where(sub > k, cols[0], 0.0)
                for b in range(blocks):
                    ms[b] = ms[b] - cols[b] * row_m
                    rs[b] = rs[b] - cols[b] * row_r
        following = []
        for (ms, rs), out in zip(states, outs):
            pivots = jnp.sum(jnp.where(sub == lane, ms[0], 0.0), axis=1, keepdims=True)
            out[pl.ds(pl.multiple_of(8 * t, 8), 8), :] = rs[0] * lax.rsqrt(pivots)
            zero = jnp.zeros((8, wide), jnp.float32)
            moved = [pltpu.roll(m, wide - 8, 1) for m in ms[1:]] + [zero]
            following.append((tuple(moved), tuple(rs[1:] + [zero])))
        return tuple(following)

    lax.fori_loop(0, blocks, body, start)


def shifted(m):
    size = m.shape[0]
    eye = lax.broadcasted_iota(jnp.int32, m.shape, 0) == lax.broadcasted_iota(jnp.int32, m.shape, 1)
    trace = jnp.sum(jnp.where(eye, m, 0.0), keepdims=True)
    return m + jnp.where(eye, (0.0001 / size) * trace, 0.0)


def mixings(grams, omega_t, outs):
    size = omega_t.shape[0]
    moments = [shifted(dot_t(dot(omega_t, g), omega_t)) for g in grams]
    eliminate([(m, omega_t) for m in moments], outs)
    lefts = [out[...] for out in outs[: len(grams)]]
    inners = []
    for left, g in zip(lefts, grams):
        hmat = dot(left, g)
        inners.append(shifted(dot_t(hmat, hmat)))
    pad = jnp.zeros((size, 128 - size), jnp.float32)
    eliminate([(c, jnp.concatenate([c, pad], axis=1)) for c in inners], outs)
    return [dot(out[:, :size], left) for out, left in zip(outs, lefts)]


def leaf_kernel(places, field_ref, gram_ref, omega_ref, packed_ref, out0):
    rows, snaps, cols = field_ref.shape
    modes = omega_ref.shape[0]
    mixing = mixings([gram_ref[...]], omega_ref[...], [out0])[0]
    width = cols // places
    per = cols // width
    lane = lax.broadcasted_iota(jnp.int32, (modes, cols), 1) // width
    for group in range(rows // per):
        pieces = [dot(mixing, field_ref[group * per + j]) for j in range(per)]
        for q in range(places):
            total = jnp.zeros((modes, cols), jnp.float32)
            for j in range(per):
                turn = (j - q) % per * width
                moved = pltpu.roll(pieces[j], turn, 1) if turn else pieces[j]
                total = jnp.where(lane == j, moved, total)
            packed_ref[q, group] = total


def leaf(places, field, gram, omega_t):
    rows, _, cols = field.shape
    modes = omega_t.shape[0]
    return pl.pallas_call(
        functools.partial(leaf_kernel, places),
        out_shape=jax.ShapeDtypeStruct((places, rows // places, modes, cols), jnp.float32),
        in_specs=[VMEM] * 3,
        out_specs=VMEM,
        scratch_shapes=[pltpu.VMEM((modes, 128), jnp.float32)],
        compiler_params=pltpu.CompilerParams(vmem_limit_bytes=VMEM_LIMIT),
    )(field, gram, omega_t)


def cross_kernel(slabs, places, packed_ref, all_ref, gram_ref, part, pieces, total, extra, *sems):
    a_send, a_recv, rs_send, rs_recv, px_send, px_recv, ag_send, ag_recv = sems
    _, groups, modes, cols = packed_ref.shape
    me = lax.axis_index("slab")
    place = lax.axis_index("param")
    count = places // 2
    share = part.shape[0] // slabs
    size = 2 * modes

    barrier = pltpu.get_barrier_semaphore()
    for k in range(1, slabs):
        pl.semaphore_signal(barrier, inc=1, device_id=(place, lax.rem(me + k, slabs)), device_id_type=MESH)
    for k in range(1, places):
        pl.semaphore_signal(barrier, inc=1, device_id=(lax.rem(place + k, places), me), device_id_type=MESH)
    pl.semaphore_wait(barrier, slabs + places - 2)

    def swap(k):
        peer = lax.rem(place + k, places)
        return pltpu.make_async_remote_copy(
            src_ref=packed_ref.at[peer], dst_ref=all_ref.at[place],
            send_sem=a_send.at[k], recv_sem=a_recv.at[k], device_id=(peer, me), device_id_type=MESH)

    for k in range(1, places):
        swap(k).start()
    for group in range(groups):
        all_ref[place, group] = packed_ref[place, group]
    for k in range(1, places):
        swap(k).wait()

    def stacked(i):
        return jnp.concatenate(
            [jnp.concatenate([all_ref[2 * i + h, g] for g in range(groups)], axis=1) for h in range(2)], axis=0)

    at = 0
    for i in range(count):
        for j in range(i, count):
            part[at * size : (at + 1) * size] = dot_t(stacked(i), stacked(j))
            at += 1

    def scatter(k):
        peer = lax.rem(me + k, slabs)
        return pltpu.make_async_remote_copy(
            src_ref=part.at[pl.ds(peer * share, share)], dst_ref=pieces.at[k],
            send_sem=rs_send.at[k], recv_sem=rs_recv.at[k], device_id=(place, peer), device_id_type=MESH)

    def across(k):
        return pltpu.make_async_remote_copy(
            src_ref=extra.at[place], dst_ref=extra.at[place],
            send_sem=px_send.at[k], recv_sem=px_recv.at[k],
            device_id=(lax.rem(place + k, places), me), device_id_type=MESH)

    def gather(k):
        peer = lax.rem(me + k, slabs)
        return pltpu.make_async_remote_copy(
            src_ref=total, dst_ref=gram_ref.at[pl.ds(me * share, share)],
            send_sem=ag_send.at[k], recv_sem=ag_recv.at[k], device_id=(place, peer), device_id_type=MESH)

    for k in range(1, slabs):
        scatter(k).start()
    acc = part[pl.ds(pl.multiple_of(me * share, 8), share)]
    for k in range(1, slabs):
        scatter(k).wait_recv()
        acc = acc + pieces[k]
    extra[place] = acc
    for k in range(1, places):
        across(k).start()
    for k in range(1, places):
        across(k).wait()
    acc = extra[0]
    for k in range(1, places):
        acc = acc + extra[k]
    total[...] = acc
    for k in range(1, slabs):
        gather(k).start()
    gram_ref[pl.ds(pl.multiple_of(me * share, 8), share)] = acc
    for k in range(1, slabs):
        scatter(k).wait_send()
    for k in range(1, slabs):
        gather(k).wait()


def cross(slabs, places, packed):
    _, groups, modes, cols = packed.shape
    count = places // 2
    tall = count * (count + 1) // 2 * 2 * modes
    share = tall // slabs
    f32 = jnp.float32
    wide = 2 * modes
    return pl.pallas_call(
        functools.partial(cross_kernel, slabs, places),
        out_shape=(jax.ShapeDtypeStruct(packed.shape, f32), jax.ShapeDtypeStruct((tall, wide), f32)),
        in_specs=[VMEM],
        out_specs=(VMEM, VMEM),
        scratch_shapes=[
            pltpu.VMEM((tall, wide), f32),
            pltpu.VMEM((slabs, share, wide), f32),
            pltpu.VMEM((share, wide), f32),
            pltpu.VMEM((places, share, wide), f32),
        ] + [pltpu.SemaphoreType.DMA((n,)) for n in (places, places, slabs, slabs, places, places, slabs, slabs)],
        compiler_params=pltpu.CompilerParams(collective_id=1, has_side_effects=True, vmem_limit_bytes=VMEM_LIMIT),
    )(packed)


def merge_kernel(all_ref, gram_ref, omega_ref, modes_ref, *outs):
    places, groups, modes, cols = all_ref.shape
    size = 2 * modes
    count = places // 2
    blocks = {}
    for i in range(count):
        for j in range(i, count):
            at = len(blocks) * size
            blocks[i, j] = gram_ref[at : at + size]
    trees = None
    level = 0
    while count:
        mixes = []
        for at in range(0, count, 2):
            some = range(at, min(at + 2, count))
            mixes += mixings([0.5 * blocks[i, i] for i in some], omega_ref[level], outs)
        mixes = [0.5**0.5 * m for m in mixes]
        if trees is None:
            trees = mixes
        else:
            trees = [
                jnp.concatenate([dot(m[:, :modes], trees[2 * i]), dot(m[:, modes:], trees[2 * i + 1])], axis=1)
                for i, m in enumerate(mixes)
            ]
        count //= 2
        level += 1
        if count:
            fine = {}
            for i in range(2 * count):
                for j in range(i, 2 * count):
                    fine[i, j] = dot_t(dot(mixes[i], blocks[i, j]), mixes[j])
            blocks = {}
            for i in range(count):
                for j in range(i, count):
                    lower = fine[2 * i + 1, 2 * j] if i < j else jnp.transpose(fine[2 * i, 2 * j + 1])
                    top = jnp.concatenate([fine[2 * i, 2 * j], fine[2 * i, 2 * j + 1]], axis=1)
                    bottom = jnp.concatenate([lower, fine[2 * i + 1, 2 * j + 1]], axis=1)
                    blocks[i, j] = jnp.concatenate([top, bottom], axis=0)
    tree = trees[0]
    for group in range(groups):
        stacked = jnp.concatenate([all_ref[i, group] for i in range(places)], axis=0)
        modes_ref[group] = dot(tree, stacked)


def merge(every, gram, omega_t):
    _, groups, modes, cols = every.shape
    return pl.pallas_call(
        merge_kernel,
        out_shape=jax.ShapeDtypeStruct((groups, modes, cols), jnp.float32),
        in_specs=[VMEM] * 3,
        out_specs=VMEM,
        scratch_shapes=[pltpu.VMEM((modes, 128), jnp.float32)] * 2,
        compiler_params=pltpu.CompilerParams(vmem_limit_bytes=VMEM_LIMIT),
    )(every, gram, omega_t)


def per_device(slabs, places, init_state, coef, source, amplitudes, sample_idx, step_counts, sketch_signs):
    _, snaps, rows, cols = init_state.shape
    signs = sketch_signs.astype(jnp.float32)
    omega_t = (2.0 * jnp.swapaxes(signs, 1, 2) - 1.0) / math.sqrt(sketch_signs.shape[1])
    field, gram = flow(slabs, init_state.reshape(snaps * rows, cols), coef[0], source,
                       amplitudes.reshape(1, -1), sample_idx, step_counts)
    packed = leaf(places, field, gram, omega_t[0])
    every, grams = cross(slabs, places, packed)
    out = merge(every, grams, omega_t[1:])
    modes = out.shape[1]
    return jnp.swapaxes(out, 0, 1).reshape(modes, rows, cols // places)


def solution(mesh):
    return jax.shard_map(
        functools.partial(per_device, mesh.shape["slab"], mesh.shape["param"]),
        mesh=mesh,
        in_specs=(
            P("param", None, "slab", None),
            P("param", "slab", None),
            P("slab", None),
            P(),
            P("param", None),
            P("param"),
            P(),
        ),
        out_specs=P(None, "slab", "param"),
        check_vma=False,
    )
```

time: 331 us -> 110 us (0.33)
  Pallas kernels: 0 us -> 105 us
  waiting for transfers between devices: 89.7 us -> 0 us
  other arithmetic: 83.8 us -> 0.91 us
  blocking collectives: 63.3 us -> 0 us
  starting transfers between devices: 50.6 us -> 0 us
  matrix products: 19 us -> 0 us
  between operations: 17.5 us -> 0.73 us
  local copies, waits for them, and re-layouts: 6.44 us -> 2.75 us
    pallas_call x0 -> x4, Pallas kernels: none -> 105 us  [the longest x1 38.5 us: flow(): pl.pallas_call(functools.partial(flow_kernel, slabs), out_shape=(jax.Shap...]
    another operation x27 -> x0, other arithmetic: 71 us -> none  [the longest x10 25.1 us: compress(): lower = jnp.linalg.cholesky(moment)]
    psum x1 -> x0, waiting for transfers between devices: 58.4 us -> none  [per_device(): gram = lax.psum(jnp.dot(stacked, stacked.T, precision=highest), 'slab')]
    psum x2 -> x0, blocking collectives: 54.9 us -> none  [per_device(): lax.psum(jnp.einsum('pac,pbc->pab', firsts, seconds, precision=highest),...]
    ppermute x16 -> x0, starting transfers between devices: 50.5 us -> none  [the longest x8 40.2 us: with_halo(): before = lax.ppermute(last, axis, up)]
    all_gather x1 -> x0, waiting for transfers between devices: 25.4 us -> none  [per_device(): lax.all_gather(piece[None], 'param', axis=0, tiled=True)]
    dot_general x25 -> x0, matrix products: 18.2 us -> none  [the longest x3 4.12 us: compress(): return (jnp.dot(mixing, stacked, precision=highest), mixing)]
    select_n x8 -> x0, other arithmetic: 11.3 us -> none  [per_device(): field = jnp.where(step < count, new, field)]
  transfers between devices with their start and end apart: 18 -> 0, of which waited for: 9 -> 0; matrix products, arithmetic and copies ran while one was open for 0% -> 0% of each run, Pallas kernels for 0% -> 0%
where the time goes in v1:
time: 110 us
  Pallas kernels  105 us (95%)
  local copies, waits for them, and re-layouts  2.75 us (2%)
    pallas_call x1, Pallas kernels, flow(): pl.pallas_call(functools.partial(flow_kernel, slabs), out_shape=(jax.Shap...  38.5 us
    pallas_call x1, Pallas kernels, merge(): pl.pallas_call(merge_kernel, out_shape=jax.ShapeDtypeStruct((groups, mode...  28.2 us
    pallas_call x1, Pallas kernels, cross(): pl.pallas_call(functools.partial(cross_kernel, slabs, places), out_shape=...  24.5 us
    pallas_call x1, Pallas kernels, leaf(): pl.pallas_call(functools.partial(leaf_kernel, places), out_shape=jax.Shap...  14.1 us

profile of v1, /device:TPU:0, one launch (start us, length us, event | category | flops | bytes accessed | tf_op | source)
XLA Modules:
  0.0 109.7 jit_solution(16035073249898392710)
XLA Ops:
  0.7 0.9 multiply_bitcast_fusion
  1.6 0.0 copy-start.1
  1.6 0.0 copy-start.2
  1.6 0.0 copy-start.3
  1.6 0.0 copy-start.4
  1.6 0.6 copy-done.1
  2.3 0.0 copy-done.2
  2.3 0.0 copy-done.3
  2.3 0.0 copy-done.4
  2.3 0.0 copy-start
  2.3 1.2 %copy-done = f32[1,128,16,128]{3,2,1,0:T(8,128)S(1)} copy-done((f32[1,128,16,128]{3,2,1,0:T(8,128)S(1)}, f32[1,128,16,128]{3,2,1,0:T(8,128)}, u32[]{:S(2)}) %copy-start) | copy-done | bytes 1048600
  3.5 38.5 %shard_map.73 = (f32[16,128,128]{2,1,0:T(8,128)S(1)}, f32[128,128]{1,0:T(8,128)S(1)}) custom-call(f32[2048,128]{1,0:T(8,128)S(1)} %bitcast.9, f32[16,128]{1,0:T(8,128)S(1)} %bitcast.11, f32[16,128]{1,0:T(8,128)S(1)} %copy-done.2, f32[1,64]{1,0:T(1,128)S(1)} %bitcast.12, s32[1,128]{1,0:T(1,128)S(1)} %copy-done.4, s32[1]{0:T(128)S(6)} %copy.9.count_ref), custom_call_target="tpu_custom_call" | custom-call | tf_op jit(solution)/shard_map/pallas_call | solution.py:169
  42.1 14.1 %shard_map.74.packed_ref = f32[4,4,64,128]{3,2,1,0:T(8,128)S(1)} custom-call(f32[16,128,128]{2,1,0:T(8,128)S(1)} %get-tuple-element.9.field_ref, f32[128,128]{1,0:T(8,128)S(1)} %get-tuple-element.10.gram_ref, f32[64,128]{1,0:T(8,128)S(1)} %slice_bitcast_fusion.omega_ref), custom_call_target="tpu_custom_call" | custom-call | tf_op jit(solution)/shard_map/pallas_call | solution.py:273
  56.2 24.5 %shard_map.75 = (f32[4,4,64,128]{3,2,1,0:T(8,128)S(1)}, f32[384,128]{1,0:T(8,128)S(1)}) custom-call(f32[4,4,64,128]{3,2,1,0:T(8,128)S(1)} %shard_map.74.packed_ref), custom_call_target="tpu_custom_call" | custom-call | tf_op jit(solution)/shard_map/pallas_call | solution.py:371
  80.7 28.2 %shard_map.76 = f32[4,64,128]{2,1,0:T(8,128)S(1)} custom-call(f32[4,4,64,128]{3,2,1,0:T(8,128)S(1)} %get-tuple-element.11.all_ref, f32[384,128]{1,0:T(8,128)S(1)} %get-tuple-element.12.gram_ref, f32[2,64,128]{2,1,0:T(8,128)S(1)} %slice.9.omega_ref), custom_call_target="tpu_custom_call" | custom-call | tf_op jit(solution)/shard_map/pallas_call | solution.py:432
  108.9 0.8 copy.8
  (2 shorter events, 0.0 us)
Async XLA Ops:
  1.6 0.7 copy-start.1
  1.6 0.7 copy-start.2
  1.6 0.7 copy-start.3
  1.6 0.7 copy-start.4
  2.3 1.2 %copy-start = (f32[1,128,16,128]{3,2,1,0:T(8,128)S(1)}, f32[1,128,16,128]{3,2,1,0:T(8,128)}, u32[]{:S(2)}) copy-start(f32[1,128,16,128]{3,2,1,0:T(8,128)} %param.7) | copy-start | bytes 3145732

commit v2 on v1

--- a/solution.py
+++ b/solution.py
@@ -9,6 +9,7 @@
 from jax.sharding import PartitionSpec as P
 
 STEPS = 8
+HALO = 2
 MESH = pl.DeviceIdType.MESH
 HIGHEST = lax.Precision.HIGHEST
 VMEM_LIMIT = 48 * 1024 * 1024
@@ -25,7 +26,7 @@
 
 
 def flow_kernel(slabs, x_ref, coef_ref, source_ref, table_ref, idx_ref, count_ref, field_ref, gram_ref,
-                buf, halo, amp_ref, part, pieces, total, halo_send, halo_recv, rs_send, rs_recv, ag_send, ag_recv):
+                buf, halo, local, nearby, amp_ref, part, pieces, total, near_send, near_recv, halo_send, halo_recv, rs_send, rs_recv, ag_send, ag_recv):
     rows, cols = coef_ref.shape
     snaps = gram_ref.shape[0]
     share = snaps // slabs
@@ -38,7 +39,7 @@
         pl.semaphore_signal(barrier, inc=1, device_id=(place, peer), device_id_type=MESH)
 
     for r in range(rows):
-        buf[0, r] = x_ref[pl.ds(r, snaps, stride=rows), :]
+        buf[0, HALO + r] = x_ref[pl.ds(r, snaps, stride=rows), :]
 
     table = jnp.broadcast_to(table_ref[...], (8, table_ref.shape[1]))
     entry = lax.broadcasted_iota(jnp.int32, (table_ref.shape[1], snaps), 0)
@@ -46,88 +47,133 @@
     amp_row = 0.1 * dot(table, picks)[0:1]
     amp_ref[...] = jnp.transpose(jnp.broadcast_to(amp_row, (cols, snaps)))
 
+    nothing = jnp.zeros((HALO, snaps, cols), jnp.float32)
+    local[0] = coef_ref[...]
+    local[1] = source_ref[...]
+
     @pl.when(me == 0)
     def _():
-        for step in range(STEPS):
-            halo[step, 0] = jnp.zeros((snaps, cols), jnp.float32)
+        nearby[0] = jnp.zeros((2, rows, cols), jnp.float32)
+        for turn in range(STEPS // HALO):
+            halo[turn, 0] = nothing
 
     @pl.when(me == slabs - 1)
     def _():
-        for step in range(STEPS):
-            halo[step, 1] = jnp.zeros((snaps, cols), jnp.float32)
+        nearby[1] = jnp.zeros((2, rows, cols), jnp.float32)
+        for turn in range(STEPS // HALO):
+            halo[turn, 1] = nothing
 
     pl.semaphore_wait(barrier, slabs - 1)
-
-    def down(step):
-        return pltpu.make_async_remote_copy(
-            src_ref=buf.at[step % 2, rows - 1], dst_ref=halo.at[step, 0],
-            send_sem=halo_send.at[step, 0], recv_sem=halo_recv.at[step, 0],
-            device_id=(place, lax.rem(me + 1, slabs)), device_id_type=MESH)
-
-    def up(step):
-        return pltpu.make_async_remote_copy(
-            src_ref=buf.at[step % 2, 0], dst_ref=halo.at[step, 1],
-            send_sem=halo_send.at[step, 1], recv_sem=halo_recv.at[step, 1],
-            device_id=(place, lax.rem(me + slabs - 1, slabs)), device_id_type=MESH)
-
-    def send(step):
+    after, before = lax.rem(me + 1, slabs), lax.rem(me + slabs - 1, slabs)
+
+    def hand(src, dst, sems, target):
+        return pltpu.make_async_remote_copy(
+            src_ref=src, dst_ref=dst, send_sem=sems[0], recv_sem=sems[1],
+            device_id=(place, target), device_id_type=MESH)
+
+    def down(turn):
+        return hand(buf.at[turn * HALO % 2, pl.ds(rows, HALO)], halo.at[turn, 0],
+                    (halo_send.at[turn, 0], halo_recv.at[turn, 0]), after)
+
+    def up(turn):
+        return hand(buf.at[turn * HALO % 2, pl.ds(HALO, HALO)], halo.at[turn, 1],
+                    (halo_send.at[turn, 1], halo_recv.at[turn, 1]), before)
+
+    def down_rates():
+        return hand(local, nearby.at[0], (near_send.at[0], near_recv.at[0]), after)
+
+    def up_rates():
+        return hand(local, nearby.at[1], (near_send.at[1], near_recv.at[1]), before)
+
+    def send(turn):
         @pl.when(me < slabs - 1)
         def _():
-            down(step).start()
+            down(turn).start()
+            if turn == 0:
+                down_rates().start()
 
         @pl.when(me > 0)
         def _():
-            up(step).start()
+            up(turn).start()
+            if turn == 0:
+                up_rates().start()
+
+    def settle(turn):
+        @pl.when(me > 0)
+        def _():
+            down(turn).wait_recv()
+            up(turn).wait_send()
+            if turn == 0:
+                down_rates().wait_recv()
+                up_rates().wait_send()
+
+        @pl.when(me < slabs - 1)
+        def _():
+            up(turn).wait_recv()
+            down(turn).wait_send()
+            if turn == 0:
+                up_rates().wait_recv()
+                down_rates().wait_send()
 
     count = count_ref[0]
     chunk = 32
     lane = lax.broadcasted_iota(jnp.int32, (chunk, cols), 1)
     first, last = lane == 0, lane == cols - 1
 
-    def update(step, r, above, below):
-        now, later = step % 2, (step + 1) % 2
+    def update(step, r, read, rates):
+        later = (step + 1) % 2
         active = jnp.where(step < count, 1.0, 0.0)
-        rate = coef_ref[pl.ds(r, 1), :] * active
-        force = source_ref[pl.ds(r, 1), :] * active
+        rate = rates[0] * active
+        force = rates[1] * active
         for c in range(0, snaps, chunk):
-            part_rows = pl.ds(c, chunk)
-            f = buf[now, r, part_rows]
+            s = pl.ds(c, chunk)
+            f = read(r, s)
             left = jnp.where(first, 0.0, pltpu.roll(f, 1, 1))
             right = jnp.where(last, 0.0, pltpu.roll(f, cols - 1, 1))
-            lap = below(part_rows) + above(part_rows) + right + left - 4.0 * f
+            lap = read(r + 1, s) + read(r - 1, s) + right + left - 4.0 * f
             th = jnp.tanh(f)
-            new = f + rate * (1.0 + 0.5 * (th * th)) * lap + amp_ref[part_rows] * force
-            buf[later, r, part_rows] = new
+            buf[later, HALO + r, s] = f + rate * (1.0 + 0.5 * (th * th)) * lap + amp_ref[s] * force
+
+    def edge(step, r):
+        turn, i = step // HALO, step % HALO
+
+        def read(at, s):
+            if i == 0 and at < 0:
+                return halo[turn, 0, HALO + at, s]
+            if i == 0 and at >= rows:
+                return halo[turn, 1, at - rows, s]
+            return buf[step % 2, HALO + at, s]
+
+        if r < 0:
+            rates = [nearby[0, n, rows + r : rows + r + 1] for n in range(2)]
+        elif r >= rows:
+            rates = [nearby[1, n, r - rows : r - rows + 1] for n in range(2)]
+        else:
+            rates = [local[n, r : r + 1] for n in range(2)]
+        update(step, r, read, rates)
 
     send(0)
-    for step in range(STEPS):
-        now = step % 2
-
-        def inner(r, carry):
-            update(step, r, lambda s: buf[now, r - 1, s], lambda s: buf[now, r + 1, s])
-            return carry
-
-        lax.fori_loop(1, rows - 1, inner, 0)
-
-        @pl.when(me > 0)
-        def _():
-            down(step).wait_recv()
-            up(step).wait_send()
-
-        @pl.when(me < slabs - 1)
-        def _():
-            up(step).wait_recv()
-            down(step).wait_send()
-
-        update(step, 0, lambda s: halo[step, 0, s], lambda s: buf[now, 1, s])
-        update(step, rows - 1, lambda s: buf[now, rows - 2, s], lambda s: halo[step, 1, s])
-        if step < STEPS - 1:
-            send(step + 1)
+    for turn in range(STEPS // HALO):
+        for i in range(HALO):
+            step = turn * HALO + i
+
+            def inner(r, carry):
+                update(step, r, lambda at, s: buf[step % 2, HALO + at, s], [local[n, pl.ds(r, 1)] for n in range(2)])
+                return carry
+
+            lax.fori_loop(1 + i, rows - 1 - i, inner, 0)
+        settle(turn)
+        for i in range(HALO):
+            step = turn * HALO + i
+            for r in list(range(i + 1 - HALO, 1 + i)) + list(range(rows - 1 - i, rows + HALO - 1 - i)):
+                edge(step, r)
+        if turn < STEPS // HALO - 1:
+            send(turn + 1)
 
     end = STEPS % 2
 
     def products(i, acc):
-        pair = jnp.concatenate([buf[end, 2 * i], buf[end, 2 * i + 1]], axis=1)
+        pair = jnp.concatenate([buf[end, HALO + 2 * i], buf[end, HALO + 2 * i + 1]], axis=1)
         return acc + dot_t(pair, pair)
 
     part[...] = lax.fori_loop(0, rows // 2, products, jnp.zeros((snaps, snaps), jnp.float32))
@@ -147,7 +193,7 @@
     for k in range(1, slabs):
         scatter(k).start()
     for r in range(rows):
-        field_ref[r] = buf[end, r]
+        field_ref[r] = buf[end, HALO + r]
     acc = part[pl.ds(pl.multiple_of(me * share, 8), share)]
     for k in range(1, slabs):
         scatter(k).wait_recv()
@@ -172,14 +218,18 @@
         in_specs=[VMEM, VMEM, VMEM, VMEM, VMEM, SMEM],
         out_specs=(VMEM, VMEM),
         scratch_shapes=[
-            pltpu.VMEM((2, rows, snaps, cols), f32),
-            pltpu.VMEM((STEPS, 2, snaps, cols), f32),
+            pltpu.VMEM((2, rows + 2 * HALO, snaps, cols), f32),
+            pltpu.VMEM((STEPS // HALO, 2, HALO, snaps, cols), f32),
+            pltpu.VMEM((2, rows, cols), f32),
+            pltpu.VMEM((2, 2, rows, cols), f32),
             pltpu.VMEM((snaps, cols), f32),
             pltpu.VMEM((snaps, snaps), f32),
             pltpu.VMEM((slabs, snaps // slabs, snaps), f32),
             pltpu.VMEM((snaps // slabs, snaps), f32),
-            pltpu.SemaphoreType.DMA((STEPS, 2)),
-            pltpu.SemaphoreType.DMA((STEPS, 2)),
+            pltpu.SemaphoreType.DMA((2,)),
+            pltpu.SemaphoreType.DMA((2,)),
+            pltpu.SemaphoreType.DMA((STEPS // HALO, 2)),
+            pltpu.SemaphoreType.DMA((STEPS // HALO, 2)),
             pltpu.SemaphoreType.DMA((slabs,)),
             pltpu.SemaphoreType.DMA((slabs,)),
             pltpu.SemaphoreType.DMA((slabs,)),
@@ -194,7 +244,6 @@
     blocks = size // 8
     wide = 128
     sub = lax.broadcasted_iota(jnp.int32, (8, wide), 0)
-    lane = lax.broadcasted_iota(jnp.int32, (8, wide), 1)
 
     def split(value):
         return tuple(value[8 * b : 8 * b + 8] for b in range(blocks))
@@ -204,25 +253,40 @@
 
     start = tuple((split(padded(m)), split(r)) for m, r in problems)
 
+    def spread(value, k):
+        return jnp.broadcast_to(value[k : k + 1], (8, wide))
+
     def body(t, carry):
-        states = [[list(ms), list(rs)] for ms, rs in carry]
+        states = []
+        for ms, rs in carry:
+            cols = [jnp.broadcast_to(ms[0][:, k : k + 1], (8, wide)) for k in range(8)]
+            zero = jnp.zeros((8, wide), jnp.float32)
+            states.append([ms[0], rs[0], cols, zero, zero])
         for k in range(8):
-            for ms, rs in states:
-                inv = 1.0 / ms[0][k : k + 1, k : k + 1]
-                row_m = ms[0][k : k + 1] * inv
-                row_r = rs[0][k : k + 1] * inv
-                cols = [jnp.broadcast_to(ms[b][:, k : k + 1], (8, wide)) for b in range(blocks)]
-                cols[0] = jnp.where(sub > k, cols[0], 0.0)
-                for b in range(blocks):
-                    ms[b] = ms[b] - cols[b] * row_m
-                    rs[b] = rs[b] - cols[b] * row_r
+            for state in states:
+                m0, r0, cols, done, scale = state
+                pivot = spread(cols[k], k)
+                inv = 1.0 / pivot
+                factor = jnp.where(sub == k, 0.0, cols[k] * inv)
+                done = jnp.where(sub == k, r0 * lax.rsqrt(pivot), done)
+                scale = jnp.where(sub == k, inv, scale)
+                cols = [c if j <= k else c - factor * spread(c, k) for j, c in enumerate(cols)]
+                state[:] = [m0 - factor * spread(m0, k), r0 - factor * spread(r0, k), cols, done, scale]
         following = []
-        for (ms, rs), out in zip(states, outs):
-            pivots = jnp.sum(jnp.where(sub == lane, ms[0], 0.0), axis=1, keepdims=True)
-            out[pl.ds(pl.multiple_of(8 * t, 8), 8), :] = rs[0] * lax.rsqrt(pivots)
+        for (ms, rs), (m0, r0, _, done, scale), out in zip(carry, states, outs):
+            out[pl.ds(pl.multiple_of(8 * t, 8), 8), :] = done
+            rows_m = [spread(m0 * scale, k) for k in range(8)]
+            rows_r = [spread(r0 * scale, k) for k in range(8)]
+            next_m, next_r = [], []
+            for m, r in zip(ms[1:], rs[1:]):
+                less_m = less_r = 0.0
+                for k in range(8):
+                    col = jnp.broadcast_to(m[:, k : k + 1], (8, wide))
+                    less_m, less_r = less_m + col * rows_m[k], less_r + col * rows_r[k]
+                next_m.append(pltpu.roll(m - less_m, wide - 8, 1))
+                next_r.append(r - less_r)
             zero = jnp.zeros((8, wide), jnp.float32)
-            moved = [pltpu.roll(m, wide - 8, 1) for m in ms[1:]] + [zero]
-            following.append((tuple(moved), tuple(rs[1:] + [zero])))
+            following.append((tuple(next_m + [zero]), tuple(next_r + [zero])))
         return tuple(following)
 
     lax.fori_loop(0, blocks, body, start)

time: 110 us -> 81.8 us (0.74)
  Pallas kernels: 105 us -> 77.2 us
    pallas_call x1, Pallas kernels: 28.2 us -> 15.5 us  [merge(): pl.pallas_call(merge_kernel, out_shape=jax.ShapeDtypeStruct((groups, mode...]
    pallas_call x1, Pallas kernels: 38.5 us -> 30.4 us  [flow(): pl.pallas_call(functools.partial(flow_kernel, slabs), out_shape=(jax.Shap...]
    pallas_call x1, Pallas kernels: 14.1 us -> 7.03 us  [leaf(): pl.pallas_call(functools.partial(leaf_kernel, places), out_shape=jax.Shap...]
where the time goes in v2:
time: 81.8 us; the launch traced here: 81.6 us
  Pallas kernels  77.2 us (94%)
  local copies, waits for them, and re-layouts  2.75 us (3%)
  other arithmetic  0.91 us (1%)
    pallas_call x1, Pallas kernels, flow(): pl.pallas_call(functools.partial(flow_kernel, slabs), out_shape=(jax.Shap...  30.4 us
    pallas_call x1, Pallas kernels, cross(): pl.pallas_call(functools.partial(cross_kernel, slabs, places), out_shape=...  24.3 us
    pallas_call x1, Pallas kernels, merge(): pl.pallas_call(merge_kernel, out_shape=jax.ShapeDtypeStruct((groups, mode...  15.5 us
    pallas_call x1, Pallas kernels, leaf(): pl.pallas_call(functools.partial(leaf_kernel, places), out_shape=jax.Shap...  7.03 us
    unnamed x10, local copies, waits for them, and re-layouts  1.9 us

profile of v2, /device:TPU:0, one launch (start us, length us, event | category | flops | bytes accessed | tf_op | source)
XLA Modules:
  0.0 81.6 jit_solution(2006675435101326072)
XLA Ops:
  0.7 0.9 %multiply_bitcast_fusion = f32[3,64,128]{2,1,0:T(8,128)S(1)} fusion(s32[3,128,64]{1,2,0:T(8,128)} %param.13), kind=kLoop, calls=%fused_computation | loop fusion | flops 98304 | bytes 196608 | tf_op jit(solution)/shard_map/div | solution.py:509
  1.6 0.0 copy-start.1
  1.6 0.0 copy-start.2
  1.6 0.0 copy-start.3
  1.6 0.0 copy-start.4
  1.6 0.6 copy-done.1
  2.3 0.0 copy-done.2
  2.3 0.0 copy-done.3
  2.3 0.0 copy-done.4
  2.3 0.0 copy-start
  2.3 1.2 %copy-done = f32[1,128,16,128]{3,2,1,0:T(8,128)S(1)} copy-done((f32[1,128,16,128]{3,2,1,0:T(8,128)S(1)}, f32[1,128,16,128]{3,2,1,0:T(8,128)}, u32[]{:S(2)}) %copy-start) | copy-done | bytes 1048600
  3.5 30.4 %shard_map.73 = (f32[16,128,128]{2,1,0:T(8,128)S(1)}, f32[128,128]{1,0:T(8,128)S(1)}) custom-call(f32[2048,128]{1,0:T(8,128)S(1)} %bitcast.9, f32[16,128]{1,0:T(8,128)S(1)} %bitcast.11, f32[16,128]{1,0:T(8,128)S(1)} %copy-done.2, f32[1,64]{1,0:T(1,128)S(1)} %bitcast.12, s32[1,128]{1,0:T(1,128)S(1)} %copy-done.4, s32[1]{0:T(128)S(6)} %copy.9.count_ref), custom_call_target="tpu_custom_call" | custom-call | tf_op jit(solution)/shard_map/pallas_call | solution.py:215
  33.9 7.0 %shard_map.74.packed_ref = f32[4,4,64,128]{3,2,1,0:T(8,128)S(1)} custom-call(f32[16,128,128]{2,1,0:T(8,128)S(1)} %get-tuple-element.9.field_ref, f32[128,128]{1,0:T(8,128)S(1)} %get-tuple-element.10.gram_ref, f32[64,128]{1,0:T(8,128)S(1)} %slice_bitcast_fusion.omega_ref), custom_call_target="tpu_custom_call" | custom-call | tf_op jit(solution)/shard_map/pallas_call | solution.py:337
  40.9 24.3 %shard_map.75 = (f32[4,4,64,128]{3,2,1,0:T(8,128)S(1)}, f32[384,128]{1,0:T(8,128)S(1)}) custom-call(f32[4,4,64,128]{3,2,1,0:T(8,128)S(1)} %shard_map.74.packed_ref), custom_call_target="tpu_custom_call" | custom-call | tf_op jit(solution)/shard_map/pallas_call | solution.py:435
  65.2 15.5 %shard_map.76 = f32[4,64,128]{2,1,0:T(8,128)S(1)} custom-call(f32[4,4,64,128]{3,2,1,0:T(8,128)S(1)} %get-tuple-element.11.all_ref, f32[384,128]{1,0:T(8,128)S(1)} %get-tuple-element.12.gram_ref, f32[2,64,128]{2,1,0:T(8,128)S(1)} %slice.9.omega_ref), custom_call_target="tpu_custom_call" | custom-call | tf_op jit(solution)/shard_map/pallas_call | solution.py:496
  80.7 0.8 %copy.8 = f32[64,4,128]{0,2,1:T(8,128)} copy(f32[64,4,128]{2,0,1:T(8,128)S(1)} %bitcast.10) | data formatting | bytes 262144 | tf_op jit(solution)/shard_map/transpose | solution.py:516
  (2 shorter events, 0.0 us)
Async XLA Ops:
  1.6 0.7 copy-start.1
  1.6 0.7 copy-start.2
  1.6 0.7 copy-start.3
  1.6 0.7 copy-start.4
  2.3 1.2 %copy-start = (f32[1,128,16,128]{3,2,1,0:T(8,128)S(1)}, f32[1,128,16,128]{3,2,1,0:T(8,128)}, u32[]{:S(2)}) copy-start(f32[1,128,16,128]{3,2,1,0:T(8,128)} %param.7) | copy-start | bytes 3145732

commit v3 on v2

--- a/solution.py
+++ b/solution.py
@@ -10,6 +10,7 @@
 
 STEPS = 8
 HALO = 2
+FUSED = False
 MESH = pl.DeviceIdType.MESH
 HIGHEST = lax.Precision.HIGHEST
 VMEM_LIMIT = 48 * 1024 * 1024
@@ -25,10 +26,19 @@
     return lax.dot_general(a, b, (((1,), (1,)), ((), ())), precision=HIGHEST, preferred_element_type=jnp.float32)
 
 
-def flow_kernel(slabs, x_ref, coef_ref, source_ref, table_ref, idx_ref, count_ref, field_ref, gram_ref,
-                buf, halo, local, nearby, amp_ref, part, pieces, total, near_send, near_recv, halo_send, halo_recv, rs_send, rs_recv, ag_send, ag_recv):
+def flow_kernel(slabs, places, x_ref, coef_ref, source_ref, table_ref, idx_ref, count_ref, omega_ref, *refs):
+    if FUSED:
+        modes_ref, every_ref, own_ref, cross_ref, *refs = refs
+    else:
+        every_ref, own_ref, cross_ref, *refs = refs
+    (buf, halo, local, nearby, amp_ref, part, pieces, total, packed, fields, grams, mixes, tall, bits, mine, extra,
+     out0, out1, near_send, near_recv, halo_send, halo_recv, rs_send, rs_recv, ag_send, ag_recv, x_send, x_recv,
+     g_send, g_recv, m_send, m_recv, rt_send, rt_recv, px_send, px_recv, at_send, at_recv) = refs
     rows, cols = coef_ref.shape
-    snaps = gram_ref.shape[0]
+    snaps = part.shape[0]
+    modes = omega_ref.shape[1]
+    groups = rows // places
+    count_pairs = places // 2
     share = snaps // slabs
     me = lax.axis_index("slab")
     place = lax.axis_index("param")
@@ -37,6 +47,8 @@
     barrier = pltpu.get_barrier_semaphore()
     for peer in peers:
         pl.semaphore_signal(barrier, inc=1, device_id=(place, peer), device_id_type=MESH)
+    for k in range(1, places):
+        pl.semaphore_signal(barrier, inc=1, device_id=(lax.rem(place + k, places), me), device_id_type=MESH)
 
     for r in range(rows):
         buf[0, HALO + r] = x_ref[pl.ds(r, snaps, stride=rows), :]
@@ -63,7 +75,7 @@
         for turn in range(STEPS // HALO):
             halo[turn, 1] = nothing
 
-    pl.semaphore_wait(barrier, slabs - 1)
+    pl.semaphore_wait(barrier, slabs + places - 2)
     after, before = lax.rem(me + 1, slabs), lax.rem(me + slabs - 1, slabs)
 
     def hand(src, dst, sems, target):
@@ -172,6 +184,39 @@
 
     end = STEPS % 2
 
+    width = cols // places
+    slot = lax.broadcasted_iota(jnp.int32, (chunk, cols), 1) // width
+
+    def pack(i, carry):
+        group = i // (snaps // chunk)
+        s = pl.ds(pl.multiple_of(i % (snaps // chunk) * chunk, chunk), chunk)
+        parts = [buf[end, HALO + group * places + j, s] for j in range(places)]
+        for q in range(places):
+            whole = parts[q]
+            for j in range(places):
+                if j != q:
+                    whole = jnp.where(slot == j, pltpu.roll(parts[j], (j - q) % places * width, 1), whole)
+            packed[q, group, s] = whole
+        return carry
+
+    lax.fori_loop(0, groups * (snaps // chunk), pack, 0)
+
+    def beside(k, src, dst, sems):
+        return pltpu.make_async_remote_copy(
+            src_ref=src, dst_ref=dst, send_sem=sems[0].at[k], recv_sem=sems[1].at[k],
+            device_id=(lax.rem(place + k, places), me), device_id_type=MESH)
+
+    def along(k, src, dst, sems):
+        return pltpu.make_async_remote_copy(
+            src_ref=src, dst_ref=dst, send_sem=sems[0].at[k], recv_sem=sems[1].at[k],
+            device_id=(place, lax.rem(me + k, slabs)), device_id_type=MESH)
+
+    def swap(k):
+        return beside(k, packed.at[lax.rem(place + k, places)], fields.at[place], (x_send, x_recv))
+
+    for k in range(1, places):
+        swap(k).start()
+
     def products(i, acc):
         pair = jnp.concatenate([buf[end, HALO + 2 * i], buf[end, HALO + 2 * i + 1]], axis=1)
         return acc + dot_t(pair, pair)
@@ -180,20 +225,15 @@
 
     def scatter(k):
         peer = lax.rem(me + k, slabs)
-        return pltpu.make_async_remote_copy(
-            src_ref=part.at[pl.ds(peer * share, share)], dst_ref=pieces.at[k],
-            send_sem=rs_send.at[k], recv_sem=rs_recv.at[k], device_id=(place, peer), device_id_type=MESH)
+        return along(k, part.at[pl.ds(peer * share, share)], pieces.at[k], (rs_send, rs_recv))
 
     def gather(k):
-        peer = lax.rem(me + k, slabs)
-        return pltpu.make_async_remote_copy(
-            src_ref=total, dst_ref=gram_ref.at[pl.ds(me * share, share)],
-            send_sem=ag_send.at[k], recv_sem=ag_recv.at[k], device_id=(place, peer), device_id_type=MESH)
+        return along(k, total, grams.at[place, pl.ds(me * share, share)], (ag_send, ag_recv))
 
     for k in range(1, slabs):
         scatter(k).start()
-    for r in range(rows):
-        field_ref[r] = buf[end, HALO + r]
+    for group in range(groups):
+        fields[place, group] = packed[place, group]
     acc = part[pl.ds(pl.multiple_of(me * share, 8), share)]
     for k in range(1, slabs):
         scatter(k).wait_recv()
@@ -201,23 +241,113 @@
     total[...] = acc
     for k in range(1, slabs):
         gather(k).start()
-    gram_ref[pl.ds(pl.multiple_of(me * share, 8), share)] = acc
+    grams[place, pl.ds(pl.multiple_of(me * share, 8), share)] = acc
+    for k in range(1, slabs):
+        gather(k).wait_recv()
+
+    def lend(k):
+        return beside(k, grams.at[place], grams.at[place], (g_send, g_recv))
+
+    def share_mix(k):
+        return beside(k, mixes.at[place], mixes.at[place], (m_send, m_recv))
+
+    for k in range(1, places):
+        lend(k).start()
+    mixes[place] = mixings([grams[place]], omega_ref[0], [out0])[0]
+    for k in range(1, places):
+        share_mix(k).start()
+    for k in range(1, places):
+        swap(k).wait_recv()
+    for k in range(1, places):
+        share_mix(k).wait_recv()
+    for i in range(places):
+        for group in range(groups):
+            every_ref[i, group] = dot(mixes[i], fields[i, group])
+
+    def piece(i):
+        return jnp.concatenate([every_ref[i, g] for g in range(groups)], axis=1)
+
+    def stacked(i):
+        return jnp.concatenate([piece(2 * i), piece(2 * i + 1)], axis=0)
+
+    at = 0
+    for i in range(count_pairs):
+        for j in range(i + 1, count_pairs):
+            tall[at : at + 2 * modes] = dot_t(stacked(i), stacked(j))
+            at += 2 * modes
+    for i in range(0, count_pairs, 2):
+        tall[at : at + modes] = jnp.concatenate(
+            [dot_t(piece(2 * h), piece(2 * h + 1)) for h in (i, i + 1)], axis=1)
+        at += modes
+    span = at // slabs
+
+    def scatter_tall(k):
+        peer = lax.rem(me + k, slabs)
+        return along(k, tall.at[pl.ds(peer * span, span)], bits.at[k], (rt_send, rt_recv))
+
+    def across(k):
+        return beside(k, extra.at[place], extra.at[place], (px_send, px_recv))
+
+    def gather_tall(k):
+        return along(k, mine, cross_ref.at[pl.ds(me * span, span)], (at_send, at_recv))
+
+    for k in range(1, slabs):
+        scatter_tall(k).start()
+    for k in range(1, places):
+        lend(k).wait_recv()
+    for i in range(places):
+        own_ref[i] = dot_t(dot(mixes[i], grams[i]), mixes[i])
+    acc = tall[pl.ds(pl.multiple_of(me * span, 8), span)]
+    for k in range(1, slabs):
+        scatter_tall(k).wait_recv()
+        acc = acc + bits[k]
+    extra[place] = acc
+    for k in range(1, places):
+        across(k).start()
+    for k in range(1, places):
+        across(k).wait_recv()
+    acc = extra[0]
+    for k in range(1, places):
+        acc = acc + extra[k]
+    mine[...] = acc
+    for k in range(1, slabs):
+        gather_tall(k).start()
+    cross_ref[pl.ds(pl.multiple_of(me * span, 8), span)] = acc
     for k in range(1, slabs):
         scatter(k).wait_send()
-    for k in range(1, slabs):
-        gather(k).wait()
-
-
-def flow(slabs, x, coef, source, table, idx, count):
+        gather(k).wait_send()
+        scatter_tall(k).wait_send()
+    for k in range(1, places):
+        swap(k).wait_send()
+        lend(k).wait_send()
+        share_mix(k).wait_send()
+        across(k).wait_send()
+    for k in range(1, slabs):
+        gather_tall(k).wait()
+    if FUSED:
+        merge_levels(every_ref, own_ref, cross_ref, omega_ref, modes_ref, out0, out1)
+
+
+def flow(slabs, places, x, coef, source, table, idx, count, omega_t):
     rows, cols = coef.shape
     snaps = x.shape[0] // rows
+    modes = omega_t.shape[1]
+    groups = rows // places
+    pairs = places // 2
+    high = pairs * (pairs - 1) // 2 * 2 * modes + pairs // 2 * modes
     f32 = jnp.float32
-    return pl.pallas_call(
-        functools.partial(flow_kernel, slabs),
-        out_shape=(jax.ShapeDtypeStruct((rows, snaps, cols), f32), jax.ShapeDtypeStruct((snaps, snaps), f32)),
-        in_specs=[VMEM, VMEM, VMEM, VMEM, VMEM, SMEM],
-        out_specs=(VMEM, VMEM),
-        scratch_shapes=[
+
+    def sems(*shape):
+        return [pltpu.SemaphoreType.DMA(shape)] * 2
+
+    inner = [(places, groups, modes, cols), (places, modes, modes), (high, 2 * modes)]
+    result = [(groups, modes, cols)] if FUSED else inner
+    out = pl.pallas_call(
+        functools.partial(flow_kernel, slabs, places),
+        out_shape=[jax.ShapeDtypeStruct(shape, f32) for shape in result],
+        in_specs=[VMEM, VMEM, VMEM, VMEM, VMEM, SMEM, VMEM],
+        out_specs=[VMEM] * len(result),
+        scratch_shapes=([pltpu.VMEM(shape, f32) for shape in inner] if FUSED else []) + [
             pltpu.VMEM((2, rows + 2 * HALO, snaps, cols), f32),
             pltpu.VMEM((STEPS // HALO, 2, HALO, snaps, cols), f32),
             pltpu.VMEM((2, rows, cols), f32),
@@ -226,17 +356,21 @@
             pltpu.VMEM((snaps, snaps), f32),
             pltpu.VMEM((slabs, snaps // slabs, snaps), f32),
             pltpu.VMEM((snaps // slabs, snaps), f32),
-            pltpu.SemaphoreType.DMA((2,)),
-            pltpu.SemaphoreType.DMA((2,)),
-            pltpu.SemaphoreType.DMA((STEPS // HALO, 2)),
-            pltpu.SemaphoreType.DMA((STEPS // HALO, 2)),
-            pltpu.SemaphoreType.DMA((slabs,)),
-            pltpu.SemaphoreType.DMA((slabs,)),
-            pltpu.SemaphoreType.DMA((slabs,)),
-            pltpu.SemaphoreType.DMA((slabs,)),
-        ],
+            pltpu.VMEM((places, groups, snaps, cols), f32),
+            pltpu.VMEM((places, groups, snaps, cols), f32),
+            pltpu.VMEM((places, snaps, snaps), f32),
+            pltpu.VMEM((places, modes, snaps), f32),
+            pltpu.VMEM((high, 2 * modes), f32),
+            pltpu.VMEM((slabs, high // slabs, 2 * modes), f32),
+            pltpu.VMEM((high // slabs, 2 * modes), f32),
+            pltpu.VMEM((places, high // slabs, 2 * modes), f32),
+            pltpu.VMEM((modes, 128), f32),
+            pltpu.VMEM((modes, 128), f32),
+        ] + sems(2) + sems(STEPS // HALO, 2) + 2 * sems(slabs) + 3 * sems(places)
+        + sems(slabs) + sems(places) + sems(slabs),
         compiler_params=pltpu.CompilerParams(collective_id=0, has_side_effects=True, vmem_limit_bytes=VMEM_LIMIT),
-    )(x, coef, source, table, idx, count)
+    )(x, coef, source, table, idx, count, omega_t)
+    return out
 
 
 def eliminate(problems, outs):
@@ -313,156 +447,31 @@
     return [dot(out[:, :size], left) for out, left in zip(outs, lefts)]
 
 
-def leaf_kernel(places, field_ref, gram_ref, omega_ref, packed_ref, out0):
-    rows, snaps, cols = field_ref.shape
-    modes = omega_ref.shape[0]
-    mixing = mixings([gram_ref[...]], omega_ref[...], [out0])[0]
-    width = cols // places
-    per = cols // width
-    lane = lax.broadcasted_iota(jnp.int32, (modes, cols), 1) // width
-    for group in range(rows // per):
-        pieces = [dot(mixing, field_ref[group * per + j]) for j in range(per)]
-        for q in range(places):
-            total = jnp.zeros((modes, cols), jnp.float32)
-            for j in range(per):
-                turn = (j - q) % per * width
-                moved = pltpu.roll(pieces[j], turn, 1) if turn else pieces[j]
-                total = jnp.where(lane == j, moved, total)
-            packed_ref[q, group] = total
-
-
-def leaf(places, field, gram, omega_t):
-    rows, _, cols = field.shape
-    modes = omega_t.shape[0]
-    return pl.pallas_call(
-        functools.partial(leaf_kernel, places),
-        out_shape=jax.ShapeDtypeStruct((places, rows // places, modes, cols), jnp.float32),
-        in_specs=[VMEM] * 3,
-        out_specs=VMEM,
-        scratch_shapes=[pltpu.VMEM((modes, 128), jnp.float32)],
-        compiler_params=pltpu.CompilerParams(vmem_limit_bytes=VMEM_LIMIT),
-    )(field, gram, omega_t)
-
-
-def cross_kernel(slabs, places, packed_ref, all_ref, gram_ref, part, pieces, total, extra, *sems):
-    a_send, a_recv, rs_send, rs_recv, px_send, px_recv, ag_send, ag_recv = sems
-    _, groups, modes, cols = packed_ref.shape
-    me = lax.axis_index("slab")
-    place = lax.axis_index("param")
-    count = places // 2
-    share = part.shape[0] // slabs
-    size = 2 * modes
-
-    barrier = pltpu.get_barrier_semaphore()
-    for k in range(1, slabs):
-        pl.semaphore_signal(barrier, inc=1, device_id=(place, lax.rem(me + k, slabs)), device_id_type=MESH)
-    for k in range(1, places):
-        pl.semaphore_signal(barrier, inc=1, device_id=(lax.rem(place + k, places), me), device_id_type=MESH)
-    pl.semaphore_wait(barrier, slabs + places - 2)
-
-    def swap(k):
-        peer = lax.rem(place + k, places)
-        return pltpu.make_async_remote_copy(
-            src_ref=packed_ref.at[peer], dst_ref=all_ref.at[place],
-            send_sem=a_send.at[k], recv_sem=a_recv.at[k], device_id=(peer, me), device_id_type=MESH)
-
-    for k in range(1, places):
-        swap(k).start()
-    for group in range(groups):
-        all_ref[place, group] = packed_ref[place, group]
-    for k in range(1, places):
-        swap(k).wait()
-
-    def stacked(i):
-        return jnp.concatenate(
-            [jnp.concatenate([all_ref[2 * i + h, g] for g in range(groups)], axis=1) for h in range(2)], axis=0)
-
-    at = 0
-    for i in range(count):
-        for j in range(i, count):
-            part[at * size : (at + 1) * size] = dot_t(stacked(i), stacked(j))
-            at += 1
-
-    def scatter(k):
-        peer = lax.rem(me + k, slabs)
-        return pltpu.make_async_remote_copy(
-            src_ref=part.at[pl.ds(peer * share, share)], dst_ref=pieces.at[k],
-            send_sem=rs_send.at[k], recv_sem=rs_recv.at[k], device_id=(place, peer), device_id_type=MESH)
-
-    def across(k):
-        return pltpu.make_async_remote_copy(
-            src_ref=extra.at[place], dst_ref=extra.at[place],
-            send_sem=px_send.at[k], recv_sem=px_recv.at[k],
-            device_id=(lax.rem(place + k, places), me), device_id_type=MESH)
-
-    def gather(k):
-        peer = lax.rem(me + k, slabs)
-        return pltpu.make_async_remote_copy(
-            src_ref=total, dst_ref=gram_ref.at[pl.ds(me * share, share)],
-            send_sem=ag_send.at[k], recv_sem=ag_recv.at[k], device_id=(place, peer), device_id_type=MESH)
-
-    for k in range(1, slabs):
-        scatter(k).start()
-    acc = part[pl.ds(pl.multiple_of(me * share, 8), share)]
-    for k in range(1, slabs):
-        scatter(k).wait_recv()
-        acc = acc + pieces[k]
-    extra[place] = acc
-    for k in range(1, places):
-        across(k).start()
-    for k in range(1, places):
-        across(k).wait()
-    acc = extra[0]
-    for k in range(1, places):
-        acc = acc + extra[k]
-    total[...] = acc
-    for k in range(1, slabs):
-        gather(k).start()
-    gram_ref[pl.ds(pl.multiple_of(me * share, 8), share)] = acc
-    for k in range(1, slabs):
-        scatter(k).wait_send()
-    for k in range(1, slabs):
-        gather(k).wait()
-
-
-def cross(slabs, places, packed):
-    _, groups, modes, cols = packed.shape
-    count = places // 2
-    tall = count * (count + 1) // 2 * 2 * modes
-    share = tall // slabs
-    f32 = jnp.float32
-    wide = 2 * modes
-    return pl.pallas_call(
-        functools.partial(cross_kernel, slabs, places),
-        out_shape=(jax.ShapeDtypeStruct(packed.shape, f32), jax.ShapeDtypeStruct((tall, wide), f32)),
-        in_specs=[VMEM],
-        out_specs=(VMEM, VMEM),
-        scratch_shapes=[
-            pltpu.VMEM((tall, wide), f32),
-            pltpu.VMEM((slabs, share, wide), f32),
-            pltpu.VMEM((share, wide), f32),
-            pltpu.VMEM((places, share, wide), f32),
-        ] + [pltpu.SemaphoreType.DMA((n,)) for n in (places, places, slabs, slabs, places, places, slabs, slabs)],
-        compiler_params=pltpu.CompilerParams(collective_id=1, has_side_effects=True, vmem_limit_bytes=VMEM_LIMIT),
-    )(packed)
-
-
-def merge_kernel(all_ref, gram_ref, omega_ref, modes_ref, *outs):
-    places, groups, modes, cols = all_ref.shape
+def merge_levels(every_ref, own_ref, cross_ref, omega_ref, modes_ref, *outs):
+    places, groups, modes, cols = every_ref.shape
     size = 2 * modes
     count = places // 2
     blocks = {}
+    at = 0
     for i in range(count):
-        for j in range(i, count):
-            at = len(blocks) * size
-            blocks[i, j] = gram_ref[at : at + size]
+        for j in range(i + 1, count):
+            blocks[i, j] = cross_ref[at : at + size]
+            at += size
+    for i in range(0, count, 2):
+        both = cross_ref[at : at + modes]
+        at += modes
+        for h in range(2):
+            inner = both[:, h * modes : (h + 1) * modes]
+            top = jnp.concatenate([own_ref[2 * (i + h)], inner], axis=1)
+            bottom = jnp.concatenate([jnp.transpose(inner), own_ref[2 * (i + h) + 1]], axis=1)
+            blocks[i + h, i + h] = jnp.concatenate([top, bottom], axis=0)
     trees = None
     level = 0
     while count:
         mixes = []
         for at in range(0, count, 2):
             some = range(at, min(at + 2, count))
-            mixes += mixings([0.5 * blocks[i, i] for i in some], omega_ref[level], outs)
+            mixes += mixings([0.5 * blocks[i, i] for i in some], omega_ref[level + 1], outs)
         mixes = [0.5**0.5 * m for m in mixes]
         if trees is None:
             trees = mixes
@@ -487,31 +496,29 @@
                     blocks[i, j] = jnp.concatenate([top, bottom], axis=0)
     tree = trees[0]
     for group in range(groups):
-        stacked = jnp.concatenate([all_ref[i, group] for i in range(places)], axis=0)
+        stacked = jnp.concatenate([every_ref[i, group] for i in range(places)], axis=0)
         modes_ref[group] = dot(tree, stacked)
 
 
-def merge(every, gram, omega_t):
+def merge(every, own, cross, omega_t):
     _, groups, modes, cols = every.shape
     return pl.pallas_call(
-        merge_kernel,
+        merge_levels,
         out_shape=jax.ShapeDtypeStruct((groups, modes, cols), jnp.float32),
-        in_specs=[VMEM] * 3,
+        in_specs=[VMEM] * 4,
         out_specs=VMEM,
         scratch_shapes=[pltpu.VMEM((modes, 128), jnp.float32)] * 2,
         compiler_params=pltpu.CompilerParams(vmem_limit_bytes=VMEM_LIMIT),
-    )(every, gram, omega_t)
+    )(every, own, cross, omega_t)
 
 
 def per_device(slabs, places, init_state, coef, source, amplitudes, sample_idx, step_counts, sketch_signs):
     _, snaps, rows, cols = init_state.shape
     signs = sketch_signs.astype(jnp.float32)
     omega_t = (2.0 * jnp.swapaxes(signs, 1, 2) - 1.0) / math.sqrt(sketch_signs.shape[1])
-    field, gram = flow(slabs, init_state.reshape(snaps * rows, cols), coef[0], source,
-                       amplitudes.reshape(1, -1), sample_idx, step_counts)
-    packed = leaf(places, field, gram, omega_t[0])
-    every, grams = cross(slabs, places, packed)
-    out = merge(every, grams, omega_t[1:])
+    parts = flow(slabs, places, init_state.reshape(snaps * rows, cols), coef[0], source,
+                 amplitudes.reshape(1, -1), sample_idx, step_counts, omega_t)
+    out = parts[0] if FUSED else merge(*parts, omega_t)
     modes = out.shape[1]
     return jnp.swapaxes(out, 0, 1).reshape(modes, rows, cols // places)
 

time: 81.8 us -> 74.7 us (0.913)
  Pallas kernels: 77.2 us -> 70.8 us
    pallas_call x4 -> x2, Pallas kernels: 77.2 us -> 70.8 us  [the longest x1 55.2 us: flow(): pl.pallas_call(functools.partial(flow_kernel, slabs, places), out_shape=[...]
where the time goes in v3:
time: 74.7 us; the launch traced here: 74.5 us
  Pallas kernels  70.8 us (95%)
  local copies, waits for them, and re-layouts  2.07 us (3%)
  other arithmetic  0.93 us (1%)
    pallas_call x1, Pallas kernels, flow(): pl.pallas_call(functools.partial(flow_kernel, slabs, places), out_shape=[...  55.2 us
    pallas_call x1, Pallas kernels, merge(): pl.pallas_call(merge_levels, out_shape=jax.ShapeDtypeStruct((groups, mode...  15.6 us

profile of v3, /device:TPU:0, one launch (start us, length us, event | category | flops | bytes accessed | tf_op | source)
XLA Modules:
  0.0 74.5 jit_solution(5465546480475029468)
XLA Ops:
  0.7 0.0 copy-start.1
  0.7 0.0 copy-start.2
  0.7 0.0 copy-start.3
  0.7 0.0 copy-start.4
  0.7 0.9 %multiply_bitcast_fusion.omega_ref = f32[3,64,128]{2,1,0:T(8,128)S(1)} fusion(s32[3,128,64]{1,2,0:T(8,128)} %param.13), kind=kLoop, calls=%fused_computation | loop fusion | flops 98304 | bytes 196608 | tf_op jit(solution)/shard_map/div | solution.py:518
  1.6 0.0 copy-done.1
  1.6 0.0 copy-done.2
  1.6 0.0 copy-done.3
  1.7 0.0 copy-done.4
  1.7 0.0 copy-start
  1.7 1.2 %copy-done = f32[1,128,16,128]{3,2,1,0:T(8,128)S(1)} copy-done((f32[1,128,16,128]{3,2,1,0:T(8,128)S(1)}, f32[1,128,16,128]{3,2,1,0:T(8,128)}, u32[]{:S(2)}) %copy-start) | copy-done | bytes 1048600
  2.9 55.2 %shard_map.73 = (f32[4,4,64,128]{3,2,1,0:T(8,128)S(1)}, f32[4,64,64]{2,1,0:T(8,128)S(1)}, f32[192,128]{1,0:T(8,128)S(1)}) custom-call(f32[2048,128]{1,0:T(8,128)S(1)} %bitcast.7, f32[16,128]{1,0:T(8,128)S(1)} %bitcast.9, f32[16,128]{1,0:T(8,128)S(1)} %copy-done.2, f32[1,64]{1,0:T(1,128)S(1)} %bitcast.10, s32[1,128]{1,0:T(1,128)S(1)} %copy-done.4, ...), custom_call_target="tpu_custom_call" | custom-call | tf_op jit(solution)/shard_map/pallas_call | solution.py:345
  58.1 15.6 %shard_map.74 = f32[4,64,128]{2,1,0:T(8,128)S(1)} custom-call(f32[4,4,64,128]{3,2,1,0:T(8,128)S(1)} %get-tuple-element.8.every_ref, f32[4,64,64]{2,1,0:T(8,128)S(1)} %get-tuple-element.9.own_ref, f32[192,128]{1,0:T(8,128)S(1)} %get-tuple-element.10.cross_ref, f32[3,64,128]{2,1,0:T(8,128)S(1)} %multiply_bitcast_fusion.omega_ref), custom_call_target="tpu_custom_call" | custom-call | tf_op jit(solution)/shard_map/pallas_call | solution.py:505
  73.7 0.8 %copy.8 = f32[64,4,128]{0,2,1:T(8,128)} copy(f32[64,4,128]{2,0,1:T(8,128)S(1)} %bitcast.8) | data formatting | bytes 262144 | tf_op jit(solution)/shard_map/transpose | solution.py:523
Async XLA Ops:
  0.7 1.0 %copy-start.1 = (f32[1,16,128]{2,1,0:T(8,128)S(1)}, f32[1,16,128]{2,1,0:T(8,128)}, u32[]{:S(2)}) copy-start(f32[1,16,128]{2,1,0:T(8,128)} %param.8) | copy-start | bytes 24580
  0.7 1.0 %copy-start.2 = (f32[16,128]{1,0:T(8,128)S(1)}, f32[16,128]{1,0:T(8,128)}, u32[]{:S(2)}) copy-start(f32[16,128]{1,0:T(8,128)} %source_ref.1) | copy-start | bytes 24580
  0.7 1.0 %copy-start.3 = (f32[64]{0:T(128)S(1)}, f32[64]{0:T(128)}, u32[]{:S(2)}) copy-start(f32[64]{0:T(128)} %param.10) | copy-start | bytes 772
  0.7 1.0 %copy-start.4 = (s32[1,128]{1,0:T(1,128)S(1)}, s32[1,128]{1,0:T(1,128)}, u32[]{:S(2)}) copy-start(s32[1,128]{1,0:T(1,128)} %idx_ref.1) | copy-start | bytes 1540
  1.7 1.2 %copy-start = (f32[1,128,16,128]{3,2,1,0:T(8,128)S(1)}, f32[1,128,16,128]{3,2,1,0:T(8,128)}, u32[]{:S(2)}) copy-start(f32[1,128,16,128]{3,2,1,0:T(8,128)} %param.7) | copy-start | bytes 3145732

commit v4 on v3

--- a/solution.py
+++ b/solution.py
@@ -9,8 +9,8 @@
 from jax.sharding import PartitionSpec as P
 
 STEPS = 8
-HALO = 2
-FUSED = False
+HALO = 4
+BATCHES = 2
 MESH = pl.DeviceIdType.MESH
 HIGHEST = lax.Precision.HIGHEST
 VMEM_LIMIT = 48 * 1024 * 1024
@@ -27,12 +27,8 @@
 
 
 def flow_kernel(slabs, places, x_ref, coef_ref, source_ref, table_ref, idx_ref, count_ref, omega_ref, *refs):
-    if FUSED:
-        modes_ref, every_ref, own_ref, cross_ref, *refs = refs
-    else:
-        every_ref, own_ref, cross_ref, *refs = refs
-    (buf, halo, local, nearby, amp_ref, part, pieces, total, packed, fields, grams, mixes, tall, bits, mine, extra,
-     out0, out1, near_send, near_recv, halo_send, halo_recv, rs_send, rs_recv, ag_send, ag_recv, x_send, x_recv,
+    (every_ref, own_ref, cross_ref, buf, halo, stage, local, nearby, amp_ref, part, pieces, total, packed, fields, grams, mixes, tall, bits, mine, extra,
+     out0, near_send, near_recv, halo_send, halo_recv, rs_send, rs_recv, ag_send, ag_recv, x_send, x_recv,
      g_send, g_recv, m_send, m_recv, rt_send, rt_recv, px_send, px_recv, at_send, at_recv) = refs
     rows, cols = coef_ref.shape
     snaps = part.shape[0]
@@ -59,7 +55,8 @@
     amp_row = 0.1 * dot(table, picks)[0:1]
     amp_ref[...] = jnp.transpose(jnp.broadcast_to(amp_row, (cols, snaps)))
 
-    nothing = jnp.zeros((HALO, snaps, cols), jnp.float32)
+    half = snaps // BATCHES
+    nothing = jnp.zeros((BATCHES, HALO, half, cols), jnp.float32)
     local[0] = coef_ref[...]
     local[1] = source_ref[...]
 
@@ -83,13 +80,11 @@
             src_ref=src, dst_ref=dst, send_sem=sems[0], recv_sem=sems[1],
             device_id=(place, target), device_id_type=MESH)
 
-    def down(turn):
-        return hand(buf.at[turn * HALO % 2, pl.ds(rows, HALO)], halo.at[turn, 0],
-                    (halo_send.at[turn, 0], halo_recv.at[turn, 0]), after)
-
-    def up(turn):
-        return hand(buf.at[turn * HALO % 2, pl.ds(HALO, HALO)], halo.at[turn, 1],
-                    (halo_send.at[turn, 1], halo_recv.at[turn, 1]), before)
+    def down(turn, b):
+        return hand(stage.at[0, b], halo.at[turn, 0, b], (halo_send.at[turn, 0, b], halo_recv.at[turn, 0, b]), after)
+
+    def up(turn, b):
+        return hand(stage.at[1, b], halo.at[turn, 1, b], (halo_send.at[turn, 1, b], halo_recv.at[turn, 1, b]), before)
 
     def down_rates():
         return hand(local, nearby.at[0], (near_send.at[0], near_recv.at[0]), after)
@@ -97,33 +92,38 @@
     def up_rates():
         return hand(local, nearby.at[1], (near_send.at[1], near_recv.at[1]), before)
 
-    def send(turn):
+    def send(turn, b):
+        now = turn * HALO % 2
+        for h in range(HALO):
+            stage[0, b, h] = buf[now, rows + h, pl.ds(b * half, half)]
+            stage[1, b, h] = buf[now, HALO + h, pl.ds(b * half, half)]
+
         @pl.when(me < slabs - 1)
         def _():
-            down(turn).start()
-            if turn == 0:
+            down(turn, b).start()
+            if turn == 0 and b == 0:
                 down_rates().start()
 
         @pl.when(me > 0)
         def _():
-            up(turn).start()
-            if turn == 0:
+            up(turn, b).start()
+            if turn == 0 and b == 0:
                 up_rates().start()
 
-    def settle(turn):
+    def settle(turn, b):
         @pl.when(me > 0)
         def _():
-            down(turn).wait_recv()
-            up(turn).wait_send()
-            if turn == 0:
+            down(turn, b).wait_recv()
+            up(turn, b).wait_send()
+            if turn == 0 and b == 0:
                 down_rates().wait_recv()
                 up_rates().wait_send()
 
         @pl.when(me < slabs - 1)
         def _():
-            up(turn).wait_recv()
-            down(turn).wait_send()
-            if turn == 0:
+            up(turn, b).wait_recv()
+            down(turn, b).wait_send()
+            if turn == 0 and b == 0:
                 up_rates().wait_recv()
                 down_rates().wait_send()
 
@@ -132,28 +132,30 @@
     lane = lax.broadcasted_iota(jnp.int32, (chunk, cols), 1)
     first, last = lane == 0, lane == cols - 1
 
-    def update(step, r, read, rates):
+    def update(step, r, read, rates, spans):
         later = (step + 1) % 2
         active = jnp.where(step < count, 1.0, 0.0)
         rate = rates[0] * active
+        half_rate = 0.5 * rate
         force = rates[1] * active
-        for c in range(0, snaps, chunk):
+        for c in spans:
             s = pl.ds(c, chunk)
             f = read(r, s)
             left = jnp.where(first, 0.0, pltpu.roll(f, 1, 1))
             right = jnp.where(last, 0.0, pltpu.roll(f, cols - 1, 1))
             lap = read(r + 1, s) + read(r - 1, s) + right + left - 4.0 * f
             th = jnp.tanh(f)
-            buf[later, HALO + r, s] = f + rate * (1.0 + 0.5 * (th * th)) * lap + amp_ref[s] * force
-
-    def edge(step, r):
+            buf[later, HALO + r, s] = f + (rate + half_rate * (th * th)) * lap + amp_ref[s] * force
+
+    def edge(step, r, b):
         turn, i = step // HALO, step % HALO
 
         def read(at, s):
+            inside = pl.ds(s.start - b * half, s.size)
             if i == 0 and at < 0:
-                return halo[turn, 0, HALO + at, s]
+                return halo[turn, 0, b, HALO + at, inside]
             if i == 0 and at >= rows:
-                return halo[turn, 1, at - rows, s]
+                return halo[turn, 1, b, at - rows, inside]
             return buf[step % 2, HALO + at, s]
 
         if r < 0:
@@ -162,25 +164,28 @@
             rates = [nearby[1, n, r - rows : r - rows + 1] for n in range(2)]
         else:
             rates = [local[n, r : r + 1] for n in range(2)]
-        update(step, r, read, rates)
-
-    send(0)
+        update(step, r, read, rates, range(b * half, (b + 1) * half, chunk))
+
+    for b in range(BATCHES):
+        send(0, b)
     for turn in range(STEPS // HALO):
         for i in range(HALO):
             step = turn * HALO + i
 
             def inner(r, carry):
-                update(step, r, lambda at, s: buf[step % 2, HALO + at, s], [local[n, pl.ds(r, 1)] for n in range(2)])
+                update(step, r, lambda at, s: buf[step % 2, HALO + at, s], [local[n, pl.ds(r, 1)] for n in range(2)],
+                       range(0, snaps, chunk))
                 return carry
 
             lax.fori_loop(1 + i, rows - 1 - i, inner, 0)
-        settle(turn)
-        for i in range(HALO):
-            step = turn * HALO + i
-            for r in list(range(i + 1 - HALO, 1 + i)) + list(range(rows - 1 - i, rows + HALO - 1 - i)):
-                edge(step, r)
-        if turn < STEPS // HALO - 1:
-            send(turn + 1)
+        for b in range(BATCHES):
+            settle(turn, b)
+            for i in range(HALO):
+                step = turn * HALO + i
+                for r in list(range(i + 1 - HALO, 1 + i)) + list(range(rows - 1 - i, rows + HALO - 1 - i)):
+                    edge(step, r, b)
+            if turn < STEPS // HALO - 1:
+                send(turn + 1, b)
 
     end = STEPS % 2
 
@@ -253,7 +258,7 @@
 
     for k in range(1, places):
         lend(k).start()
-    mixes[place] = mixings([grams[place]], omega_ref[0], [out0])[0]
+    mixes[place] = mixings([grams[place]], omega_rows(omega_ref[0]), [out0])[0]
     for k in range(1, places):
         share_mix(k).start()
     for k in range(1, places):
@@ -324,9 +329,6 @@
         across(k).wait_send()
     for k in range(1, slabs):
         gather_tall(k).wait()
-    if FUSED:
-        merge_levels(every_ref, own_ref, cross_ref, omega_ref, modes_ref, out0, out1)
-
 
 def flow(slabs, places, x, coef, source, table, idx, count, omega_t):
     rows, cols = coef.shape
@@ -340,16 +342,16 @@
     def sems(*shape):
         return [pltpu.SemaphoreType.DMA(shape)] * 2
 
-    inner = [(places, groups, modes, cols), (places, modes, modes), (high, 2 * modes)]
-    result = [(groups, modes, cols)] if FUSED else inner
-    out = pl.pallas_call(
+    result = [(places, groups, modes, cols), (places, modes, modes), (high, 2 * modes)]
+    return pl.pallas_call(
         functools.partial(flow_kernel, slabs, places),
         out_shape=[jax.ShapeDtypeStruct(shape, f32) for shape in result],
         in_specs=[VMEM, VMEM, VMEM, VMEM, VMEM, SMEM, VMEM],
         out_specs=[VMEM] * len(result),
-        scratch_shapes=([pltpu.VMEM(shape, f32) for shape in inner] if FUSED else []) + [
+        scratch_shapes=[
             pltpu.VMEM((2, rows + 2 * HALO, snaps, cols), f32),
-            pltpu.VMEM((STEPS // HALO, 2, HALO, snaps, cols), f32),
+            pltpu.VMEM((STEPS // HALO, 2, BATCHES, HALO, snaps // BATCHES, cols), f32),
+            pltpu.VMEM((2, BATCHES, HALO, snaps // BATCHES, cols), f32),
             pltpu.VMEM((2, rows, cols), f32),
             pltpu.VMEM((2, 2, rows, cols), f32),
             pltpu.VMEM((snaps, cols), f32),
@@ -365,12 +367,10 @@
             pltpu.VMEM((high // slabs, 2 * modes), f32),
             pltpu.VMEM((places, high // slabs, 2 * modes), f32),
             pltpu.VMEM((modes, 128), f32),
-            pltpu.VMEM((modes, 128), f32),
-        ] + sems(2) + sems(STEPS // HALO, 2) + 2 * sems(slabs) + 3 * sems(places)
+        ] + sems(2) + sems(STEPS // HALO, 2, BATCHES) + 2 * sems(slabs) + 3 * sems(places)
         + sems(slabs) + sems(places) + sems(slabs),
         compiler_params=pltpu.CompilerParams(collective_id=0, has_side_effects=True, vmem_limit_bytes=VMEM_LIMIT),
     )(x, coef, source, table, idx, count, omega_t)
-    return out
 
 
 def eliminate(problems, outs):
@@ -426,6 +426,10 @@
     lax.fori_loop(0, blocks, body, start)
 
 
+def omega_rows(signs):
+    return (2.0 * signs.astype(jnp.float32) - 1.0) / math.sqrt(signs.shape[1])
+
+
 def shifted(m):
     size = m.shape[0]
     eye = lax.broadcasted_iota(jnp.int32, m.shape, 0) == lax.broadcasted_iota(jnp.int32, m.shape, 1)
@@ -450,6 +454,7 @@
 def merge_levels(every_ref, own_ref, cross_ref, omega_ref, modes_ref, *outs):
     places, groups, modes, cols = every_ref.shape
     size = 2 * modes
+    width = cols // places
     count = places // 2
     blocks = {}
     at = 0
@@ -471,7 +476,7 @@
         mixes = []
         for at in range(0, count, 2):
             some = range(at, min(at + 2, count))
-            mixes += mixings([0.5 * blocks[i, i] for i in some], omega_ref[level + 1], outs)
+            mixes += mixings([0.5 * blocks[i, i] for i in some], omega_rows(omega_ref[level + 1]), outs)
         mixes = [0.5**0.5 * m for m in mixes]
         if trees is None:
             trees = mixes
@@ -497,14 +502,16 @@
     tree = trees[0]
     for group in range(groups):
         stacked = jnp.concatenate([every_ref[i, group] for i in range(places)], axis=0)
-        modes_ref[group] = dot(tree, stacked)
+        whole = jnp.transpose(dot(tree, stacked))
+        for j in range(places):
+            modes_ref[group * places + j] = whole[j * width : (j + 1) * width]
 
 
 def merge(every, own, cross, omega_t):
-    _, groups, modes, cols = every.shape
+    places, groups, modes, cols = every.shape
     return pl.pallas_call(
         merge_levels,
-        out_shape=jax.ShapeDtypeStruct((groups, modes, cols), jnp.float32),
+        out_shape=jax.ShapeDtypeStruct((groups * places, cols // places, modes), jnp.float32),
         in_specs=[VMEM] * 4,
         out_specs=VMEM,
         scratch_shapes=[pltpu.VMEM((modes, 128), jnp.float32)] * 2,
@@ -514,13 +521,11 @@
 
 def per_device(slabs, places, init_state, coef, source, amplitudes, sample_idx, step_counts, sketch_signs):
     _, snaps, rows, cols = init_state.shape
-    signs = sketch_signs.astype(jnp.float32)
-    omega_t = (2.0 * jnp.swapaxes(signs, 1, 2) - 1.0) / math.sqrt(sketch_signs.shape[1])
+    signs = jnp.swapaxes(sketch_signs, 1, 2)
     parts = flow(slabs, places, init_state.reshape(snaps * rows, cols), coef[0], source,
-                 amplitudes.reshape(1, -1), sample_idx, step_counts, omega_t)
-    out = parts[0] if FUSED else merge(*parts, omega_t)
-    modes = out.shape[1]
-    return jnp.swapaxes(out, 0, 1).reshape(modes, rows, cols // places)
+                 amplitudes.reshape(1, -1), sample_idx, step_counts, signs)
+    out = merge(*parts, signs)
+    return jnp.transpose(out, (2, 0, 1))
 
 
 def solution(mesh):

time: 74.7 us -> 72.9 us (0.976)
  Pallas kernels: 70.8 us -> 68.5 us
  local copies, waits for them, and re-layouts: 2.07 us -> 3.47 us
  other arithmetic: 0.93 us -> 0 us
    pallas_call x1, Pallas kernels: 55.2 us -> 52 us  [flow(): pl.pallas_call(functools.partial(flow_kernel, slabs, places), out_shape=[...]
    unnamed x10 -> x12, local copies, waits for them, and re-layouts: 1.24 us -> 3.47 us
    div x1 -> x0, other arithmetic: 0.93 us -> none  [per_device(): (2.0 * jnp.swapaxes(signs, 1, 2) - 1.0) / math.sqrt(sketch_signs.shape[1])]
    transpose x1 -> x0, local copies, waits for them, and re-layouts: 0.84 us -> none  [per_device(): return jnp.swapaxes(out, 0, 1).reshape(modes, rows, cols // places)]
    pallas_call x1, Pallas kernels: 15.6 us -> 16.4 us  [merge(): pl.pallas_call(merge_levels, out_shape=jax.ShapeDtypeStruct((groups * pla...]
where the time goes in v4:
time: 72.9 us; the launch traced here: 72.6 us
  Pallas kernels  68.5 us (94%)
  local copies, waits for them, and re-layouts  3.47 us (5%)
    pallas_call x1, Pallas kernels, flow(): pl.pallas_call(functools.partial(flow_kernel, slabs, places), out_shape=[...  52 us
    pallas_call x1, Pallas kernels, merge(): pl.pallas_call(merge_levels, out_shape=jax.ShapeDtypeStruct((groups * pla...  16.4 us
    unnamed x12, local copies, waits for them, and re-layouts  3.47 us

profile of v4, /device:TPU:0, one launch (start us, length us, event | category | flops | bytes accessed | tf_op | source)
XLA Modules:
  0.0 72.6 jit_solution(10977241268662829677)
XLA Ops:
  0.0 0.0 copy-start.2
  0.7 0.0 copy-start.4
  0.7 0.0 copy-start.5
  0.7 0.0 copy-done.2
  0.7 0.6 copy-done.4
  1.3 0.0 copy-done.5
  1.3 0.0 copy-start
  1.3 1.2 %copy-done = f32[1,128,16,128]{3,2,1,0:T(8,128)S(1)} copy-done((f32[1,128,16,128]{3,2,1,0:T(8,128)S(1)}, f32[1,128,16,128]{3,2,1,0:T(8,128)}, u32[]{:S(2)}) %copy-start) | copy-done | bytes 1048600
  2.6 0.0 copy-start.1
  2.6 0.9 %copy-done.1 = s32[3,128,64]{1,2,0:T(8,128)S(1)} copy-done((s32[3,128,64]{1,2,0:T(8,128)S(1)}, s32[3,128,64]{1,2,0:T(8,128)}, u32[]{:S(2)}) %copy-start.1) | copy-done | bytes 98328
  3.5 0.0 copy-start.3
  3.5 0.7 copy-done.3
  4.2 52.0 %shard_map.73 = (f32[4,4,64,128]{3,2,1,0:T(8,128)S(1)}, f32[4,64,64]{2,1,0:T(8,128)S(1)}, f32[192,128]{1,0:T(8,128)S(1)}) custom-call(f32[2048,128]{1,0:T(8,128)S(1)} %bitcast.5, f32[16,128]{1,0:T(8,128)S(1)} %bitcast.8, f32[16,128]{1,0:T(8,128)S(1)} %copy-done.3, f32[1,64]{1,0:T(1,128)S(1)} %bitcast.9, s32[1,128]{1,0:T(1,128)S(1)} %copy-done.5, ...), custom_call_target="tpu_custom_call" | custom-call | tf_op jit(solution)/shard_map/pallas_call | solution.py:346
  56.2 16.4 %shard_map.74 = f32[16,32,64]{2,1,0:T(8,128)} custom-call(f32[4,4,64,128]{3,2,1,0:T(8,128)S(1)} %get-tuple-element.8.every_ref, f32[4,64,64]{2,1,0:T(8,128)S(1)} %get-tuple-element.9.own_ref, f32[192,128]{1,0:T(8,128)S(1)} %get-tuple-element.10.cross_ref, s32[3,64,128]{2,1,0:T(8,128)S(1)} %bitcast.7), custom_call_target="tpu_custom_call" | custom-call | tf_op jit(solution)/shard_map/pallas_call | solution.py:512
Async XLA Ops:
  0.0 0.7 copy-start.2
  0.7 0.7 copy-start.4
  0.7 0.7 copy-start.5
  1.3 1.2 %copy-start = (f32[1,128,16,128]{3,2,1,0:T(8,128)S(1)}, f32[1,128,16,128]{3,2,1,0:T(8,128)}, u32[]{:S(2)}) copy-start(f32[1,128,16,128]{3,2,1,0:T(8,128)} %param.7) | copy-start | bytes 3145732
  2.6 0.9 %copy-start.1 = (s32[3,128,64]{1,2,0:T(8,128)S(1)}, s32[3,128,64]{1,2,0:T(8,128)}, u32[]{:S(2)}) copy-start(s32[3,128,64]{1,2,0:T(8,128)} %param.13) | copy-start | bytes 294916
  3.5 0.7 copy-start.3

commit v5 on v4

--- a/solution.py
+++ b/solution.py
@@ -9,12 +9,13 @@
 from jax.sharding import PartitionSpec as P
 
 STEPS = 8
-HALO = 4
+HALO = 2
 BATCHES = 2
 MESH = pl.DeviceIdType.MESH
 HIGHEST = lax.Precision.HIGHEST
-VMEM_LIMIT = 48 * 1024 * 1024
+VMEM_LIMIT = 63 * 1024 * 1024
 VMEM = pl.BlockSpec(memory_space=pltpu.VMEM)
+HBM = pl.BlockSpec(memory_space=pltpu.HBM)
 SMEM = pl.BlockSpec(memory_space=pltpu.SMEM)
 
 
@@ -26,13 +27,13 @@
     return lax.dot_general(a, b, (((1,), (1,)), ((), ())), precision=HIGHEST, preferred_element_type=jnp.float32)
 
 
-def flow_kernel(slabs, places, x_ref, coef_ref, source_ref, table_ref, idx_ref, count_ref, omega_ref, *refs):
-    (every_ref, own_ref, cross_ref, buf, halo, stage, local, nearby, amp_ref, part, pieces, total, packed, fields, grams, mixes, tall, bits, mine, extra,
+def flow_kernel(slabs, places, x_far, coef_ref, source_far, table_far, idx_far, count_ref, signs_far, *refs):
+    (every_ref, own_ref, cross_ref, x_ref, table_ref, idx_ref, signs_ref, load_sem, buf, halo, stage, local, nearby, amp_ref, part, pieces, total, packed, fields, grams, mixes, tall, bits, mine, extra,
      out0, near_send, near_recv, halo_send, halo_recv, rs_send, rs_recv, ag_send, ag_recv, x_send, x_recv,
      g_send, g_recv, m_send, m_recv, rt_send, rt_recv, px_send, px_recv, at_send, at_recv) = refs
     rows, cols = coef_ref.shape
     snaps = part.shape[0]
-    modes = omega_ref.shape[1]
+    modes = signs_ref.shape[0]
     groups = rows // places
     count_pairs = places // 2
     share = snaps // slabs
@@ -40,12 +41,23 @@
     place = lax.axis_index("param")
     peers = [lax.rem(me + k, slabs) for k in range(1, slabs)]
 
+    loads = [
+        pltpu.make_async_copy(src, dst, load_sem.at[n])
+        for n, (src, dst) in enumerate([
+            (x_far, x_ref), (coef_ref, local.at[0]), (source_far, local.at[1]),
+            (table_far, table_ref), (idx_far, idx_ref), (signs_far.at[0], signs_ref)])
+    ]
+    for load in loads:
+        load.start()
+
     barrier = pltpu.get_barrier_semaphore()
     for peer in peers:
         pl.semaphore_signal(barrier, inc=1, device_id=(place, peer), device_id_type=MESH)
     for k in range(1, places):
         pl.semaphore_signal(barrier, inc=1, device_id=(lax.rem(place + k, places), me), device_id_type=MESH)
 
+    for load in loads:
+        load.wait()
     for r in range(rows):
         buf[0, HALO + r] = x_ref[pl.ds(r, snaps, stride=rows), :]
 
@@ -57,8 +69,6 @@
 
     half = snaps // BATCHES
     nothing = jnp.zeros((BATCHES, HALO, half, cols), jnp.float32)
-    local[0] = coef_ref[...]
-    local[1] = source_ref[...]
 
     @pl.when(me == 0)
     def _():
@@ -258,7 +268,7 @@
 
     for k in range(1, places):
         lend(k).start()
-    mixes[place] = mixings([grams[place]], omega_rows(omega_ref[0]), [out0])[0]
+    mixes[place] = mixings([grams[place]], omega_rows(signs_ref[...]), [out0])[0]
     for k in range(1, places):
         share_mix(k).start()
     for k in range(1, places):
@@ -346,9 +356,14 @@
     return pl.pallas_call(
         functools.partial(flow_kernel, slabs, places),
         out_shape=[jax.ShapeDtypeStruct(shape, f32) for shape in result],
-        in_specs=[VMEM, VMEM, VMEM, VMEM, VMEM, SMEM, VMEM],
+        in_specs=[HBM, HBM, HBM, HBM, HBM, SMEM, HBM],
         out_specs=[VMEM] * len(result),
         scratch_shapes=[
+            pltpu.VMEM(x.shape, f32),
+            pltpu.VMEM(table.shape, f32),
+            pltpu.VMEM(idx.shape, jnp.int32),
+            pltpu.VMEM(omega_t.shape[1:], jnp.int32),
+            pltpu.SemaphoreType.DMA((6,)),
             pltpu.VMEM((2, rows + 2 * HALO, snaps, cols), f32),
             pltpu.VMEM((STEPS // HALO, 2, BATCHES, HALO, snaps // BATCHES, cols), f32),
             pltpu.VMEM((2, BATCHES, HALO, snaps // BATCHES, cols), f32),
@@ -395,19 +410,23 @@
         for ms, rs in carry:
             cols = [jnp.broadcast_to(ms[0][:, k : k + 1], (8, wide)) for k in range(8)]
             zero = jnp.zeros((8, wide), jnp.float32)
-            states.append([ms[0], rs[0], cols, zero, zero])
+            states.append([ms[0], rs[0], cols, zero, zero, spread(cols[0], 0)])
         for k in range(8):
             for state in states:
-                m0, r0, cols, done, scale = state
-                pivot = spread(cols[k], k)
+                m0, r0, cols, done, scale, pivot = state
                 inv = 1.0 / pivot
-                factor = jnp.where(sub == k, 0.0, cols[k] * inv)
                 done = jnp.where(sub == k, r0 * lax.rsqrt(pivot), done)
                 scale = jnp.where(sub == k, inv, scale)
-                cols = [c if j <= k else c - factor * spread(c, k) for j, c in enumerate(cols)]
-                state[:] = [m0 - factor * spread(m0, k), r0 - factor * spread(r0, k), cols, done, scale]
+                hidden = jnp.where(sub == k, 0.0, cols[k])
+                heads = [spread(c, k) if j > k else None for j, c in enumerate(cols)]
+                if k < 7:
+                    pivot = spread(cols[k + 1], k + 1) - spread(cols[k], k + 1) * heads[k + 1] * inv
+                cols = [c if j <= k else c - hidden * heads[j] * inv for j, c in enumerate(cols)]
+                m0 = m0 - hidden * spread(m0, k) * inv
+                r0 = r0 - hidden * spread(r0, k) * inv
+                state[:] = [m0, r0, cols, done, scale, pivot]
         following = []
-        for (ms, rs), (m0, r0, _, done, scale), out in zip(carry, states, outs):
+        for (ms, rs), (m0, r0, _, done, scale, _), out in zip(carry, states, outs):
             out[pl.ds(pl.multiple_of(8 * t, 8), 8), :] = done
             rows_m = [spread(m0 * scale, k) for k in range(8)]
             rows_r = [spread(r0 * scale, k) for k in range(8)]

time: 72.9 us -> 73.2 us (level)
  Pallas kernels: 68.5 us -> 72.4 us
  local copies, waits for them, and re-layouts: 3.47 us -> 0 us
    unnamed x12 -> x0, local copies, waits for them, and re-layouts: 3.47 us -> none
    pallas_call x1, Pallas kernels: 52 us -> 54.8 us  [flow(): pl.pallas_call(functools.partial(flow_kernel, slabs, places), out_shape=[...]
    pallas_call x1, Pallas kernels: 16.4 us -> 17.6 us  [merge(): pl.pallas_call(merge_levels, out_shape=jax.ShapeDtypeStruct((groups * pla...]
where the time goes in v5:
time: 73.2 us; the launch traced here: 73 us
  Pallas kernels  72.4 us (99%)
    pallas_call x1, Pallas kernels, flow(): pl.pallas_call(functools.partial(flow_kernel, slabs, places), out_shape=[...  54.8 us
    pallas_call x1, Pallas kernels, merge(): pl.pallas_call(merge_levels, out_shape=jax.ShapeDtypeStruct((groups * pla...  17.6 us

profile of v5, /device:TPU:0, one launch (start us, length us, event | category | flops | bytes accessed | tf_op | source)
XLA Modules:
  0.0 73.0 jit_solution(17835711643464890857)
XLA Ops:
  0.7 54.8 %shard_map.73 = (f32[4,4,64,128]{3,2,1,0:T(8,128)}, f32[4,64,64]{2,1,0:T(8,128)}, f32[192,128]{1,0:T(8,128)}) custom-call(f32[2048,128]{1,0:T(8,128)} %bitcast.5, f32[16,128]{1,0:T(8,128)} %bitcast.8, f32[16,128]{1,0:T(8,128)} %source_far.1, f32[1,64]{1,0:T(1,128)} %bitcast.9, s32[1,128]{1,0:T(1,128)} %idx_far.1, s32[1]{0:T(128)S(6)} %copy.8.count_ref, ...), custom_call_target="tpu_custom_call" | custom-call | tf_op jit(solution)/shard_map/pallas_call | solution.py:356
  55.4 17.6 %shard_map.74 = f32[16,32,64]{2,1,0:T(8,128)} custom-call(f32[4,4,64,128]{3,2,1,0:T(8,128)} %get-tuple-element.8.every_ref, f32[4,64,64]{2,1,0:T(8,128)} %get-tuple-element.9.own_ref, f32[192,128]{1,0:T(8,128)} %get-tuple-element.10.cross_ref, s32[3,64,128]{2,1,0:T(8,128)} %bitcast.7), custom_call_target="tpu_custom_call" | custom-call | tf_op jit(solution)/shard_map/pallas_call | solution.py:531

commit v6 on v5

--- a/solution.py
+++ b/solution.py
@@ -28,12 +28,12 @@
 
 
 def flow_kernel(slabs, places, x_far, coef_ref, source_far, table_far, idx_far, count_ref, signs_far, *refs):
-    (every_ref, own_ref, cross_ref, x_ref, table_ref, idx_ref, signs_ref, load_sem, buf, halo, stage, local, nearby, amp_ref, part, pieces, total, packed, fields, grams, mixes, tall, bits, mine, extra,
-     out0, near_send, near_recv, halo_send, halo_recv, rs_send, rs_recv, ag_send, ag_recv, x_send, x_recv,
+    (modes_ref, every_ref, own_ref, cross_ref, x_ref, table_ref, idx_ref, signs_ref, load_sem, buf, halo, stage, local, nearby, amp_ref, part, pieces, total, packed, fields, grams, mixes, tall, bits, mine, extra,
+     out0, out1, near_send, near_recv, halo_send, halo_recv, rs_send, rs_recv, ag_send, ag_recv, x_send, x_recv,
      g_send, g_recv, m_send, m_recv, rt_send, rt_recv, px_send, px_recv, at_send, at_recv) = refs
     rows, cols = coef_ref.shape
     snaps = part.shape[0]
-    modes = signs_ref.shape[0]
+    modes = signs_ref.shape[1]
     groups = rows // places
     count_pairs = places // 2
     share = snaps // slabs
@@ -45,7 +45,7 @@
         pltpu.make_async_copy(src, dst, load_sem.at[n])
         for n, (src, dst) in enumerate([
             (x_far, x_ref), (coef_ref, local.at[0]), (source_far, local.at[1]),
-            (table_far, table_ref), (idx_far, idx_ref), (signs_far.at[0], signs_ref)])
+            (table_far, table_ref), (idx_far, idx_ref), (signs_far, signs_ref)])
     ]
     for load in loads:
         load.start()
@@ -268,7 +268,7 @@
 
     for k in range(1, places):
         lend(k).start()
-    mixes[place] = mixings([grams[place]], omega_rows(signs_ref[...]), [out0])[0]
+    mixes[place] = mixings([grams[place]], omega_rows(signs_ref[0]), [out0])[0]
     for k in range(1, places):
         share_mix(k).start()
     for k in range(1, places):
@@ -339,6 +339,7 @@
         across(k).wait_send()
     for k in range(1, slabs):
         gather_tall(k).wait()
+    merge_levels(every_ref, own_ref, cross_ref, signs_ref, modes_ref, out0, out1)
 
 def flow(slabs, places, x, coef, source, table, idx, count, omega_t):
     rows, cols = coef.shape
@@ -352,17 +353,17 @@
     def sems(*shape):
         return [pltpu.SemaphoreType.DMA(shape)] * 2
 
-    result = [(places, groups, modes, cols), (places, modes, modes), (high, 2 * modes)]
+    inner = [(places, groups, modes, cols), (places, modes, modes), (high, 2 * modes)]
     return pl.pallas_call(
         functools.partial(flow_kernel, slabs, places),
-        out_shape=[jax.ShapeDtypeStruct(shape, f32) for shape in result],
+        out_shape=jax.ShapeDtypeStruct((rows, cols // places, modes), f32),
         in_specs=[HBM, HBM, HBM, HBM, HBM, SMEM, HBM],
-        out_specs=[VMEM] * len(result),
-        scratch_shapes=[
+        out_specs=VMEM,
+        scratch_shapes=[pltpu.VMEM(shape, f32) for shape in inner] + [
             pltpu.VMEM(x.shape, f32),
             pltpu.VMEM(table.shape, f32),
             pltpu.VMEM(idx.shape, jnp.int32),
-            pltpu.VMEM(omega_t.shape[1:], jnp.int32),
+            pltpu.VMEM(omega_t.shape, jnp.int32),
             pltpu.SemaphoreType.DMA((6,)),
             pltpu.VMEM((2, rows + 2 * HALO, snaps, cols), f32),
             pltpu.VMEM((STEPS // HALO, 2, BATCHES, HALO, snaps // BATCHES, cols), f32),
@@ -381,6 +382,7 @@
             pltpu.VMEM((slabs, high // slabs, 2 * modes), f32),
             pltpu.VMEM((high // slabs, 2 * modes), f32),
             pltpu.VMEM((places, high // slabs, 2 * modes), f32),
+            pltpu.VMEM((modes, 128), f32),
             pltpu.VMEM((modes, 128), f32),
         ] + sems(2) + sems(STEPS // HALO, 2, BATCHES) + 2 * sems(slabs) + 3 * sems(places)
         + sems(slabs) + sems(places) + sems(slabs),
@@ -526,24 +528,11 @@
             modes_ref[group * places + j] = whole[j * width : (j + 1) * width]
 
 
-def merge(every, own, cross, omega_t):
-    places, groups, modes, cols = every.shape
-    return pl.pallas_call(
-        merge_levels,
-        out_shape=jax.ShapeDtypeStruct((groups * places, cols // places, modes), jnp.float32),
-        in_specs=[VMEM] * 4,
-        out_specs=VMEM,
-        scratch_shapes=[pltpu.VMEM((modes, 128), jnp.float32)] * 2,
-        compiler_params=pltpu.CompilerParams(vmem_limit_bytes=VMEM_LIMIT),
-    )(every, own, cross, omega_t)
-
-
 def per_device(slabs, places, init_state, coef, source, amplitudes, sample_idx, step_counts, sketch_signs):
     _, snaps, rows, cols = init_state.shape
     signs = jnp.swapaxes(sketch_signs, 1, 2)
-    parts = flow(slabs, places, init_state.reshape(snaps * rows, cols), coef[0], source,
-                 amplitudes.reshape(1, -1), sample_idx, step_counts, signs)
-    out = merge(*parts, signs)
+    out = flow(slabs, places, init_state.reshape(snaps * rows, cols), coef[0], source,
+               amplitudes.reshape(1, -1), sample_idx, step_counts, signs)
     return jnp.transpose(out, (2, 0, 1))
 
 

time: 73.2 us -> 72.9 us (level)
  Pallas kernels: 72.4 us -> 70.4 us
  local copies, waits for them, and re-layouts: 0 us -> 1.67 us
    pallas_call x2 -> x1, Pallas kernels: 72.4 us -> 70.4 us  [flow(): pl.pallas_call(functools.partial(flow_kernel, slabs, places), out_shape=j...]
    unnamed x0 -> x1, local copies, waits for them, and re-layouts: none -> 1.67 us
where the time goes in v6:
time: 72.9 us; the launch traced here: 72.7 us
  Pallas kernels  70.4 us (97%)
  local copies, waits for them, and re-layouts  1.67 us (2%)
    pallas_call x1, Pallas kernels, flow(): pl.pallas_call(functools.partial(flow_kernel, slabs, places), out_shape=j...  70.4 us
    unnamed x1, local copies, waits for them, and re-layouts  1.67 us

profile of v6, /device:TPU:0, one launch (start us, length us, event | category | flops | bytes accessed | tf_op | source)
XLA Modules:
  0.0 72.7 jit_solution(4680882526801769924)
XLA Ops:
  0.7 70.4 %shard_map.73 = f32[16,32,64]{2,1,0:T(8,128)} custom-call(f32[2048,128]{1,0:T(8,128)} %bitcast.5, f32[16,128]{1,0:T(8,128)} %bitcast.8, f32[16,128]{1,0:T(8,128)} %source_far.1, f32[1,64]{1,0:T(1,128)} %bitcast.9, s32[1,128]{1,0:T(1,128)} %idx_far.1, s32[1]{0:T(128)S(6)} %copy.9.count_ref, s32[3,64,128]{2,1,0:T(8,128)} %bitcast.7), custom_call_target="tpu_custom_call" | custom-call | tf_op jit(solution)/shard_map/pallas_call | solution.py:357
  71.0 1.7 %copy.10 = f32[64,16,32]{0,2,1:T(8,128)} copy(f32[64,16,32]{0,2,1:T(8,128)} %bitcast.6) | data formatting | bytes 262144
